TPU v7x, 128 devices: a whole 4x4x4 slice. The times are simulated.
128 devices in a mesh: seq: 16 (over y_hi, z, core), fsdp: 8 (over x, y_lo).
Axes of the slice: x: 4, y: 4 (y_hi: 2, y_lo: 2; y = y_hi * 2 + y_lo), z: 4, core: 2. Of those that a mesh axis runs over, the one named last changes fastest.
Arguments:
- tokens: bfloat16 [8, 2048, 4096], P('fsdp', 'seq'), may hold values from -40 to 40
- cotangent: bfloat16 [8, 2048, 4096], P('fsdp', 'seq'), may hold values from -6 to 6
- w_query: bfloat16 [4096, 2048], P(None, 'fsdp'), may hold values from -0.09375 to 0.09375
- w_key: bfloat16 [4096, 2048], P(None, 'fsdp'), may hold values from -0.09375 to 0.09375
- w_value: bfloat16 [4096, 2048], P(None, 'fsdp'), may hold values from -0.09375 to 0.09375
- w_output: bfloat16 [2048, 4096], P('fsdp'), may hold values from -0.125 to 0.125
- global_pos: int32 [8, 128], replicated, may hold values from 0 to 2047
- pattern: int32 [8, 32, 2], P(None, 'seq'), may hold values 0 or 1
Outputs:
- grad_tokens: bfloat16 [8, 2048, 4096], P('fsdp', 'seq')
- grad_query: float32 [4096, 2048], P('seq', 'fsdp')
- grad_key: float32 [4096, 2048], P('seq', 'fsdp')
- grad_value: float32 [4096, 2048], P('seq', 'fsdp')
- grad_output: float32 [2048, 4096], P('fsdp', 'seq')
All inputs are finite; a program needn't handle non-finite values. No bound on the sum of `pattern` on one device may be relied on, other than what follows from the above.
Results may differ from a plain program's by a relative error of at most 0.019.
Values may be sent and summed in bfloat16 or wider, within the bound.
A program may use at most 192 MiB of HBM per device.

v0:
```python
import jax
import jax.numpy as jnp
from jax import lax
from jax.sharding import PartitionSpec as P

HDIM = 128
BLOCK = 64


def with_halo(value, sides, width):
    for axis, dim in sides:
        devices, length = (lax.axis_size(axis), value.shape[dim])
        up = [(i, (i + 1) % devices) for i in range(devices - 1)]
        down = [(j, i) for i, j in up]
        last = lax.slice_in_dim(value, length - width, length, axis=dim)
        leading = lax.slice_in_dim(value, 0, width, axis=dim)
        before = lax.ppermute(last, axis, up)
        after = lax.ppermute(leading, axis, down)
        value = jnp.concatenate([before, value, after], axis=dim)
    return value


def product(form, left, right):
    return jnp.einsum(form, left, right, preferred_element_type=jnp.float32)


def block_mask(pattern, first_block, block_total):
    block_count = pattern.shape[0]
    index = first_block + jnp.arange(block_count, dtype=jnp.int32)
    before = (pattern[:, 0] == 1) & (index > 0)
    after = (pattern[:, 1] == 1) & (index < block_total - 1)
    middle = jnp.ones((block_count, BLOCK), jnp.bool_)
    return jnp.concatenate(
        [
            jnp.broadcast_to(before[:, None], (block_count, BLOCK)),
            middle,
            jnp.broadcast_to(after[:, None], (block_count, BLOCK)),
        ],
        axis=1,
    )


def windows(extended, block_count):
    blocks = extended.reshape(block_count + 2, BLOCK, extended.shape[-1])
    return jnp.concatenate([blocks[:block_count], blocks[1 : block_count + 1], blocks[2:]], axis=1)


def unwindow(grads, block_count):
    lower = grads[:, :BLOCK]
    center = grads[:, BLOCK : 2 * BLOCK]
    upper = grads[:, 2 * BLOCK :]
    summed = jnp.pad(lower, ((0, 2), (0, 0), (0, 0))) + jnp.pad(center, ((1, 1), (0, 0), (0, 0)))
    summed = summed + jnp.pad(upper, ((2, 0), (0, 0), (0, 0)))
    return summed.reshape((block_count + 2) * BLOCK, grads.shape[-1])


def doc_attention(query, extended, global_kv, pattern, grad_ctx, first_block, block_total):
    row_count, head_width = query.shape
    block_count = row_count // BLOCK
    head_count = head_width // HDIM
    scale = HDIM ** (-0.5)
    window_kv = windows(extended, block_count)
    key_win = window_kv[..., :head_width].reshape(block_count, 3 * BLOCK, head_count, HDIM)
    value_win = window_kv[..., head_width:].reshape(block_count, 3 * BLOCK, head_count, HDIM)
    key_glob = global_kv[:, :head_width].reshape(-1, head_count, HDIM)
    value_glob = global_kv[:, head_width:].reshape(-1, head_count, HDIM)
    queries = query.reshape(block_count, BLOCK, head_count, HDIM)
    grad_out = grad_ctx.reshape(block_count, BLOCK, head_count, HDIM)
    mask = block_mask(pattern, first_block, block_total)
    local = product("nqhe,nkhe->nhqk", queries, key_win) * scale
    local = jnp.where(mask[:, None, None, :], local, -jnp.inf)
    remote = product("nqhe,ghe->nhqg", queries, key_glob) * scale
    top = jnp.maximum(local.max(-1), remote.max(-1))[..., None]
    local_exp = jnp.exp(local - top)
    remote_exp = jnp.exp(remote - top)
    denom = local_exp.sum(-1, keepdims=True) + remote_exp.sum(-1, keepdims=True)
    p_local = local_exp / denom
    p_remote = remote_exp / denom
    p_local_b = p_local.astype(jnp.bfloat16)
    p_remote_b = p_remote.astype(jnp.bfloat16)
    context = (
        product("nhqk,nkhe->nqhe", p_local_b, value_win)
        + product("nhqg,ghe->nqhe", p_remote_b, value_glob)
    ).astype(jnp.bfloat16)
    d_local = product("nqhe,nkhe->nhqk", grad_out, value_win)
    d_remote = product("nqhe,ghe->nhqg", grad_out, value_glob)
    delta = (p_local * d_local).sum(-1, keepdims=True) + (p_remote * d_remote).sum(
        -1, keepdims=True
    )
    s_local = (p_local * (d_local - delta) * scale).astype(jnp.bfloat16)
    s_remote = (p_remote * (d_remote - delta) * scale).astype(jnp.bfloat16)
    grad_q = (
        product("nhqk,nkhe->nqhe", s_local, key_win) + product("nhqg,ghe->nqhe", s_remote, key_glob)
    ).astype(jnp.bfloat16)
    dkey_win = product("nhqk,nqhe->nkhe", s_local, queries)
    dvalue_win = product("nhqk,nqhe->nkhe", p_local_b, grad_out)
    dkey_glob = product("nhqg,nqhe->ghe", s_remote, queries)
    dvalue_glob = product("nhqg,nqhe->ghe", p_remote_b, grad_out)
    grad_ext = unwindow(
        jnp.concatenate(
            [
                dkey_win.reshape(block_count, 3 * BLOCK, head_width),
                dvalue_win.reshape(block_count, 3 * BLOCK, head_width),
            ],
            -1,
        ),
        block_count,
    )
    grad_glob = jnp.concatenate(
        [dkey_glob.reshape(-1, head_width), dvalue_glob.reshape(-1, head_width)], -1
    )
    return (
        context.reshape(row_count, head_width),
        grad_q.reshape(row_count, head_width),
        grad_ext,
        grad_glob,
    )


def contract_rows(left, right):
    return lax.dot_general(
        left, right, (((0,), (0,)), ((), ())), preferred_element_type=jnp.float32
    )


def contract_cols(left, right):
    return lax.dot_general(
        left, right, (((1,), (1,)), ((), ())), preferred_element_type=jnp.float32
    )


def on_device(tokens, cotangent, w_query, w_key, w_value, w_output, global_pos, pattern):
    inputs = lax.all_gather(tokens, "fsdp", axis=0, tiled=True)
    doc_count, row_count, model_width = inputs.shape
    head_width = w_query.shape[1]
    flat = inputs.reshape(doc_count * row_count, model_width)
    query = jnp.dot(flat, w_query, preferred_element_type=jnp.float32).astype(jnp.bfloat16)
    keys = jnp.dot(flat, w_key, preferred_element_type=jnp.float32).astype(jnp.bfloat16)
    value_rows = jnp.dot(flat, w_value, preferred_element_type=jnp.float32).astype(jnp.bfloat16)
    keys_vals = jnp.concatenate([keys, value_rows], -1).reshape(
        doc_count, row_count, 2 * head_width
    )
    extended = with_halo(keys_vals, (("seq", 1),), BLOCK)
    seq_start = lax.axis_index("seq") * row_count
    selector = (
        global_pos[:, :, None] - seq_start == jnp.arange(row_count, dtype=jnp.int32)[None, None, :]
    )
    picked = jnp.einsum(
        "bgt,btc->bgc", selector.astype(jnp.bfloat16), keys_vals, preferred_element_type=jnp.float32
    )
    global_kv = lax.psum(picked.astype(jnp.bfloat16), "seq")
    grads_in = lax.all_gather(cotangent, "fsdp", axis=0, tiled=True)
    grads_flat = grads_in.reshape(doc_count * row_count, model_width)
    grad_ctx = contract_cols(grads_flat, w_output).astype(jnp.bfloat16)
    block_count = row_count // BLOCK
    first_block = lax.axis_index("seq") * block_count
    block_total = block_count * lax.axis_size("seq")
    context, grad_q, grad_ext, grad_glob = jax.vmap(
        doc_attention, in_axes=(0, 0, 0, 0, 0, None, None)
    )(
        query.reshape(doc_count, row_count, head_width),
        extended,
        global_kv,
        pattern,
        grad_ctx.reshape(doc_count, row_count, head_width),
        first_block,
        block_total,
    )
    rims = jnp.concatenate([grad_ext[:, :BLOCK], grad_ext[:, row_count + BLOCK :]], 1)
    received = with_halo(rims, (("seq", 1),), BLOCK)
    owned = grad_ext[:, BLOCK : row_count + BLOCK]
    owned = owned + jnp.pad(received[:, :BLOCK], ((0, 0), (0, row_count - BLOCK), (0, 0)))
    owned = owned + jnp.pad(received[:, 3 * BLOCK :], ((0, 0), (row_count - BLOCK, 0), (0, 0)))
    glob_sum = lax.psum(grad_glob, "seq")
    owned = owned + jnp.einsum(
        "bgt,bgc->btc", selector.astype(jnp.float32), glob_sum, precision=lax.Precision.HIGHEST
    )
    flat_q = grad_q.reshape(doc_count * row_count, head_width)
    flat_k = owned[..., :head_width].astype(jnp.bfloat16).reshape(doc_count * row_count, head_width)
    flat_v = owned[..., head_width:].astype(jnp.bfloat16).reshape(doc_count * row_count, head_width)
    flat_ctx = context.reshape(doc_count * row_count, head_width)
    partial_value = (
        contract_cols(flat_q, w_query)
        + contract_cols(flat_k, w_key)
        + contract_cols(flat_v, w_value)
    ).reshape(doc_count, row_count, model_width)
    grad_tokens = lax.psum_scatter(
        partial_value.astype(jnp.bfloat16), "fsdp", scatter_dimension=0, tiled=True
    )
    whole_term = jnp.concatenate(
        [
            contract_rows(flat, flat_q),
            contract_rows(flat, flat_k),
            contract_rows(flat, flat_v),
            contract_rows(grads_flat, flat_ctx),
        ],
        1,
    )
    shares = lax.psum_scatter(
        whole_term.astype(jnp.bfloat16), "seq", scatter_dimension=0, tiled=True
    ).astype(jnp.float32)
    grad_query = shares[:, :head_width]
    grad_key = shares[:, head_width : 2 * head_width]
    grad_value = shares[:, 2 * head_width : 3 * head_width]
    grad_output = shares[:, 3 * head_width :].T
    return (grad_tokens, grad_query, grad_key, grad_value, grad_output)


def solution(mesh):
    in_specs = (
        P("fsdp", "seq", None),
        P("fsdp", "seq", None),
        P(None, "fsdp"),
        P(None, "fsdp"),
        P(None, "fsdp"),
        P("fsdp", None),
        P(),
        P(None, "seq", None),
    )
    out_specs = (
        P("fsdp", "seq", None),
        P("seq", "fsdp"),
        P("seq", "fsdp"),
        P("seq", "fsdp"),
        P("fsdp", "seq"),
    )
    return jax.shard_map(
        on_device, mesh=mesh, in_specs=in_specs, out_specs=out_specs, check_vma=False
    )
```

profile of v0, /device:TPU:1, one launch (start us, length us, event | category | flops | bytes accessed | tf_op | source)
XLA Modules:
  0.0 1004.6 jit_solution(13753035469822413667)
XLA Ops:
  9.3 171.9 %all-gather.3.cloned.1.call-done = bf16[8,128,4096]{2,1,0:T(8,128)(2,1)} async-done(((bf16[1,128,4096]{2,1,0:T(8,128)(2,1)}), bf16[8,128,4096]{2,1,0:T(8,128)(2,1)}) %all-gather.3.cloned.1.call-update) | async-done | bytes 8388624 | tf_op jit(solution)/shard_map/all_gather | solution.py:133
  181.3 6.5 convolution_convert_fusion.5
  194.2 3.7 collective-permute-start
  199.9 6.5 convolution_convert_fusion.4
  206.4 150.2 %all-gather.5.cloned.1.call-done = bf16[8,128,4096]{2,1,0:T(8,128)(2,1)} async-done(((bf16[1,128,4096]{2,1,0:T(8,128)(2,1)}), bf16[8,128,4096]{2,1,0:T(8,128)(2,1)}) %all-gather.5.cloned.1.call-update) | async-done | bytes 8388624 | tf_op jit(solution)/shard_map/all_gather | solution.py:152
  356.6 7.2 convolution_convert_fusion.3
  381.2 141.3 %all-reduce.8.cloned.1.call-done = bf16[8,128,512]{2,1,0:T(8,128)(2,1)} async-done(((bf16[8,128,512]{2,1,0:T(8,128)(2,1)}), bf16[8,128,512]{2,1,0:T(8,128)(2,1)}) %all-reduce.8.cloned.1.call-update) | async-done | bytes 1048592 | tf_op jit(solution)/shard_map/psum | solution.py:151
  533.8 3.0 convolution_bitcast_fusion.2
  548.7 2.5 copy.199
  557.0 3.2 pad_maximum_fusion.3
  571.6 3.4 collective-permute-start.3
  575.1 3.9 fusion.3
  579.0 3.7 fusion.2
  582.8 2.7 collective-permute-done.2
  585.5 4.5 collective-permute-done.3
  590.0 116.1 %all-reduce.10.cloned.1.call-done = f32[8,128,512]{2,1,0:T(8,128)} async-done(((f32[8,128,512]{2,1,0:T(8,128)}), f32[8,128,512]{2,1,0:T(8,128)}) %all-reduce.10.cloned.1.call-update) | async-done | bytes 2097168 | tf_op jit(solution)/shard_map/psum | solution.py:174
  706.1 4.3 fusion.8
  710.4 5.9 fusion.4
  718.8 4.0 pad_maximum_fusion
  723.1 9.3 fusion.40
  734.2 9.8 fusion.82
  743.9 17.2 %add_convert_fusion = bf16[1024,4096]{1,0:T(8,128)(2,1)} fusion(f32[1024,4096]{1,0:T(8,128)} %fusion.40, f32[1024,4096]{1,0:T(8,128)} %fusion.82, bf16[1024,256]{1,0:T(8,128)(2,1)S(1)} %bitcast.191, bf16[4096,256]{1,0:T(8,128)(2,1)} %param.12), kind=kOutput, calls=%fused_computation | convolution fusion | flops 2160066560 | bytes 44564480 | tf_op jit(solution)/shard_map/dot_general | solution.py:127
  761.2 64.3 %reduce-scatter.5.cloned.1.call-done = bf16[256,1024]{0,1:T(8,128)(2,1)} async-done(((bf16[4096,1024]{0,1:T(8,128)(2,1)}), bf16[256,1024]{0,1:T(8,128)(2,1)}) %reduce-scatter.5.cloned.1.call-update) | async-done | bytes 524304 | tf_op jit(solution)/shard_map/reduce_scatter | solution.py:199
  830.0 167.5 %reduce-scatter.3.cloned.1.call-done = bf16[1,128,4096]{2,1,0:T(8,128)(2,1)} async-done(((bf16[8,128,4096]{2,1,0:T(8,128)(2,1)}), bf16[1,128,4096]{2,1,0:T(8,128)(2,1)}) %reduce-scatter.3.cloned.1.call-update) | async-done | bytes 1048592 | tf_op jit(solution)/shard_map/reduce_scatter | solution.py:187
  (160 shorter events, 76.8 us)
Async XLA Ops:
  7.2 192.7 %copy-start = (bf16[4096,256]{1,0:T(8,128)(2,1)S(1)}, bf16[4096,256]{1,0:T(8,128)(2,1)}, u32[]{:S(2)}) copy-start(bf16[4096,256]{1,0:T(8,128)(2,1)} %param.10) | copy-start | bytes 6291460
  7.2 174.1 %all-gather.3.cloned.1.call-start = ((), (), s32[]{:S(2)}) async-start(), calls=%async_computation.2 | async-start | bytes 9437184 | tf_op jit(solution)/shard_map/all_gather | solution.py:133
  7.9 348.7 %all-gather.5.cloned.1.call-start = ((), (), s32[]{:S(2)}) async-start(), calls=%async_computation.4 | async-start | bytes 9437184 | tf_op jit(solution)/shard_map/all_gather | solution.py:152
  8.7 513.8 %all-reduce.8.cloned.1.call-start = ((), (), s32[]{:S(2)}) async-start(), calls=%async_computation.3 | async-start | bytes 2097152 | tf_op jit(solution)/shard_map/psum | solution.py:151
  181.3 6.5 copy-start.1
  181.3 7.0 copy-start.22
  194.2 179.5 %collective-permute-start = (bf16[8,64,512]{2,1,0:T(8,128)(2,1)}, bf16[8,64,512]{2,1,0:T(8,128)(2,1)}, u32[]{:S(2)}, u32[]{:S(2)}) collective-permute-start(bf16[8,64,512]{2,1,0:T(8,128)(2,1)} %get-tuple-element.48), channel_id=1, source_target_pairs={{0,8},{8,16},{16,24},{24,32},{32,40},{40,48},{48,56},{56,64},{64,7... | collective-permute-start | bytes 1572872 | tf_op jit(solution)/shard_map/ppermute | solution.py:17
  198.0 175.7 %collective-permute-start.1 = (bf16[8,64,512]{2,1,0:T(8,128)(2,1)}, bf16[8,64,512]{2,1,0:T(8,128)(2,1)}, u32[]{:S(2)}, u32[]{:S(2)}) collective-permute-start(bf16[8,64,512]{2,1,0:T(8,128)(2,1)} %get-tuple-element.49), channel_id=1, source_target_pairs={{8,0},{16,8},{24,16},{32,24},{40,32},{48,40},{56,48},{64,56},{72,6... | collective-permute-start | bytes 1572872 | tf_op jit(solution)/shard_map/ppermute | solution.py:18
  373.2 332.9 %all-reduce.10.cloned.1.call-start = ((), (), s32[]{:S(2)}) async-start(), calls=%async_computation.5 | async-start | bytes 4194304 | tf_op jit(solution)/shard_map/psum | solution.py:174
  381.2 143.8 %copy-start.26 = (bf16[8,2,64,2,128]{4,2,1,3,0:T(8,128)(2,1)S(1)}, bf16[8,2,64,2,128]{4,2,1,3,0:T(8,128)(2,1)}, u32[]{:S(2)}) copy-start(bf16[8,2,64,2,128]{4,2,1,3,0:T(8,128)(2,1)} %copy.171) | copy-start | bytes 1572868
  560.2 265.3 %reduce-scatter.5.cloned.1.call-start = ((), (), s32[]{:S(2)}) async-start(), calls=%async_computation.7 | async-start | bytes 8912896 | tf_op jit(solution)/shard_map/reduce_scatter | solution.py:199
  565.5 9.5 slice-start.4
  566.1 12.9 %copy-start.11 = (bf16[8,2,64,2,128]{4,3,2,1,0:T(2,128)(2,1)}, bf16[8,2,64,2,128]{4,3,2,1,0:T(2,128)(2,1)S(1)}, u32[]{:S(2)}) copy-start(bf16[8,2,64,2,128]{4,3,2,1,0:T(2,128)(2,1)S(1)} %copy.191) | copy-start | bytes 1572868
  566.1 9.0 slice-start.5
  566.1 9.0 copy-start.19
  567.2 11.8 %slice-start = ((s8[8388608]{0:T(1024)(128)(4,1)}), s8[4194304]{0:T(1024)(128)(4,1)S(1)}, s32[]{:S(2)}) async-start(s8[8388608]{0:T(1024)(128)(4,1)} %bitcast.167), calls=%async_computation.8 | async-start | bytes 8388608
  569.3 16.1 %collective-permute-start.2 = (f32[8,64,512]{2,1,0:T(8,128)S(1)}, f32[8,64,512]{2,1,0:T(8,128)}, u32[]{:S(2)}, u32[]{:S(2)}) collective-permute-start(f32[8,64,512]{2,1,0:T(8,128)S(1)} %get-tuple-element.35), channel_id=1, source_target_pairs={{0,8},{8,16},{16,24},{24,32},{32,40},{40,48},{48,56},{56,64},{64,7... | collective-permute-start | bytes 3145736 | tf_op jit(solution)/shard_map/ppermute | solution.py:17
  571.6 18.3 %collective-permute-start.3 = (f32[8,64,512]{2,1,0:T(8,128)S(1)}, f32[8,64,512]{2,1,0:T(8,128)}, u32[]{:S(2)}, u32[]{:S(2)}) collective-permute-start(f32[8,64,512]{2,1,0:T(8,128)S(1)} %get-tuple-element.36), channel_id=1, source_target_pairs={{8,0},{16,8},{24,16},{32,24},{40,32},{48,40},{56,48},{64,56},{72,6... | collective-permute-start | bytes 3145736 | tf_op jit(solution)/shard_map/ppermute | solution.py:18
  575.1 3.9 slice-start.1
  706.1 10.2 %slice-start.2 = ((s8[8388608]{0:T(1024)(128)(4,1)}), s8[4194304]{0:T(1024)(128)(4,1)S(1)}, s32[]{:S(2)}) async-start(s8[8388608]{0:T(1024)(128)(4,1)} %bitcast.170), calls=%async_computation.10 | async-start | bytes 8388608
  710.4 5.9 slice-start.3
  722.8 274.7 %reduce-scatter.3.cloned.1.call-start = ((), (), s32[]{:S(2)}) async-start(), calls=%async_computation.6 | async-start | bytes 9437184 | tf_op jit(solution)/shard_map/reduce_scatter | solution.py:187
  734.2 9.8 copy-start.21
  825.5 3.7 copy-start.18
  (22 other events, 40.0 us)
Sparse Core Ops, SparseCore 0:
  9.7 171.5 all-gather.2
  182.9 173.6 all-gather.4
  373.3 149.1 all-reduce.7
  560.3 145.7 all-reduce.9
  722.9 102.5 reduce-scatter.4
  828.5 168.9 reduce-scatter.2
where the time goes:
time: 1010 us; the launch traced here: 1000 us
  waiting for transfers between devices  820 us (81%)
  matrix products  99.9 us (10%)
  local copies, waits for them, and re-layouts  40.9 us (4%)
  other arithmetic  16.4 us (2%)
  between operations  15 us (1%)
  starting transfers between devices  12.5 us (1%)
    all_gather x1, waiting for transfers between devices, on_device(): inputs = lax.all_gather(tokens, 'fsdp', axis=0, tiled=True)  172 us
    reduce_scatter x1, waiting for transfers between devices, on_device(): lax.psum_scatter(partial_value.astype(jnp.bfloat16), 'fsdp', scatter_dime...  168 us
    all_gather x1, waiting for transfers between devices, on_device(): grads_in = lax.all_gather(cotangent, 'fsdp', axis=0, tiled=True)  150 us
    psum x1, waiting for transfers between devices, on_device(): global_kv = lax.psum(picked.astype(jnp.bfloat16), 'seq')  141 us
    psum x1, waiting for transfers between devices, on_device(): glob_sum = lax.psum(grad_glob, 'seq')  116 us
    reduce_scatter x1, waiting for transfers between devices, on_device(): lax.psum_scatter(whole_term.astype(jnp.bfloat16), 'seq', scatter_dimensio...  64.3 us
    dot_general x4, matrix products, contract_cols(): lax.dot_general(left, right, (((1,), (1,)), ((), ())), preferred_element_...  43.5 us
  transfers between devices with their start and end apart: 10, of which 8 were waited for; matrix products, arithmetic and copies ran while one was open for 10% of the time, Pallas kernels for 0%

commit v1 on v0

v1 whole, which is shorter than its diff:
```python
import jax
import jax.numpy as jnp
from jax import lax
from jax.experimental import pallas as pl
from jax.experimental.pallas import tpu as pltpu
from jax.sharding import PartitionSpec as P

BLOCK = 64
HDIM = 128
ROWS = 128
CHIP_ROWS = 256
D = 4096
BF = jnp.bfloat16
F32 = jnp.float32
MESH = pl.DeviceIdType.MESH
ANY = pl.BlockSpec(memory_space=pl.ANY)
NT = (((1,), (1,)), ((), ()))
TN = (((0,), (0,)), ((), ()))


def place():
    f = lax.axis_index("fsdp")
    s = lax.axis_index("seq")
    x, p = lax.div(f, 2), lax.rem(f, 2)
    yh, z, c = lax.div(s, 8), lax.rem(lax.div(s, 2), 4), lax.rem(s, 2)
    return x, 2 * yh + p, z, c


def device(x, y, z, c):
    return {"seq": lax.div(y, 2) * 8 + z * 2 + c, "fsdp": x * 2 + lax.rem(y, 2)}


def mod4(v):
    return lax.rem(v + 4, 4)


def al(v, n):
    return pl.multiple_of(v, n)


def remote(src, dst, send, recv, where):
    return pltpu.make_async_remote_copy(
        src_ref=src, dst_ref=dst, send_sem=send, recv_sem=recv, device_id=where, device_id_type=MESH
    )


def meet(devices):
    barrier = pltpu.get_barrier_semaphore()
    for where in devices:
        pl.semaphore_signal(barrier, inc=1, device_id=where, device_id_type=MESH)
    pl.semaphore_wait(barrier, len(devices))


def chip_peer(x, y, z, c, k):
    j = lax.rem(lax.div(y, 2) * 4 + z + k, 8)
    return j, device(x, lax.div(j, 4) * 2 + lax.rem(y, 2), lax.rem(j, 4), c)


def gather_kernel(
    tok_in, cot_in, wq, wk, wv, wo,
    tok_out, cot_out, w_out, r_out,
    tok, cot, w, wov, stage,
    ssem, rsem, wssem, wrsem, lsem, assem, arsem, bssem, brsem, osem,
):
    x, y, z, c = place()
    p = lax.rem(y, 2)
    xr, xl, x2 = mod4(x + 1), mod4(x - 1), mod4(x + 2)
    right, left = device(xr, y, z, c), device(xl, y, z, c)
    sib = device(x, y, z, 1 - c)
    me = lax.div(y, 2) * 4 + z
    peers = [chip_peer(x, y, z, c, k) for k in range(1, 8)]
    up, down = mod4(y + 1), mod4(y - 1)
    meet(
        [right, left, sib]
        + [device(x, v, z, core) for v in (up, down) for core in (0, 1)]
        + [where for _, where in peers]
    )
    own = pl.ds(al(c * ROWS, ROWS), ROWS)
    first = pl.ds(al(c * ROWS, 64), 64)
    second = pl.ds(al(c * ROWS + 64, 64), 64)

    def sends(a, given, buf):
        def cp(kind, src, dst, where):
            return remote(src, dst, ssem.at[a, kind], rsem.at[a, kind], where)

        return [
            cp(0, given, buf.at[x, own], right),
            cp(1, given, buf.at[x, own], left),
            cp(2, given, buf.at[x, own], sib),
            cp(3, buf.at[xl, first], buf.at[xl, first], right),
            cp(4, buf.at[xr, second], buf.at[xr, second], left),
            cp(5, buf.at[xl, own], buf.at[xl, own], sib),
            cp(6, buf.at[xr, own], buf.at[xr, own], sib),
            cp(7, buf.at[x2, first], buf.at[x2, first], sib),
            cp(8, buf.at[x2, second], buf.at[x2, second], sib),
        ]

    tsend = sends(0, tok_in, tok)
    csend = sends(1, cot_in, cot)
    ydst = mod4(y + 1 + 2 * c)
    wdev = device(x, ydst, z, p)
    half = pl.ds(al(c * 2048, 2048), 2048)
    half_o = pl.ds(al(c * 128, 128), 128)
    wsend = [
        remote(src.at[half], w.at[t, half], wssem.at[t], wrsem.at[t, c], wdev)
        for t, src in enumerate((wq, wk, wv))
    ]
    wsend.append(remote(wo.at[half_o], wov.at[half_o], wssem.at[3], wrsem.at[3, c], wdev))
    wlocal = [pltpu.make_async_copy(src, w.at[t], lsem.at[t]) for t, src in enumerate((wq, wk, wv))]
    wlocal.append(pltpu.make_async_copy(wo, wov, lsem.at[3]))
    tlocal = pltpu.make_async_copy(tok_in, tok.at[x, own], lsem.at[4])
    clocal = pltpu.make_async_copy(cot_in, cot.at[x, own], lsem.at[5])

    for k in (0, 1, 2):
        tsend[k].start()
    for cp in wsend:
        cp.start()
    tlocal.start()
    clocal.start()

    @pl.when(c == p)
    def _():
        for cp in wlocal:
            cp.start()

    def relay(copies):
        copies[0].wait_recv()
        copies[3].start()
        copies[5].start()
        copies[1].wait_recv()
        copies[4].start()
        copies[6].start()

    relay(tsend)
    for k in (0, 1, 2):
        csend[k].start()
    tsend[3].wait_recv()
    tsend[7].start()
    tsend[4].wait_recv()
    tsend[8].start()
    tlocal.wait()
    clocal.wait()

    def weights_here(ts):
        @pl.when(c == p)
        def _():
            for t in ts:
                wlocal[t].wait()

        @pl.when(c != p)
        def _():
            for t in ts:
                for h in (0, 1):
                    if t < 3:
                        ref = w.at[t, pl.ds(h * 2048, 2048)]
                    else:
                        ref = wov.at[pl.ds(h * 128, 128)]
                    remote(ref, ref, wssem.at[t], wrsem.at[t, h], sib).wait_recv()

    weights_here((0, 1, 2))
    for k in (2, 5, 6, 7, 8):
        tsend[k].wait_recv()
    out_t = pltpu.make_async_copy(tok, tok_out, osem.at[0])
    out_t.start()
    out_w = pltpu.make_async_copy(w, w_out, osem.at[2])
    out_w.start()

    @pl.loop(0, 4)
    def _(doc):
        @pl.loop(0, 3)
        def _(t):
            got = jnp.dot(tok[doc], w[t], preferred_element_type=F32).astype(BF)
            stage[2 * doc, t] = got[:, :HDIM]
            stage[2 * doc + 1, t] = got[:, HDIM:]

    mine = pl.ds(al(me * CHIP_ROWS, CHIP_ROWS), CHIP_ROWS)
    qkv = [
        remote(stage.at[j, pl.ds(0, 3)], r_out.at[pl.ds(0, 3), mine], assem.at[k], arsem.at[k], where)
        for k, (j, where) in enumerate(peers)
    ]
    for cp in qkv:
        cp.start()
    qkv_own = pltpu.make_async_copy(stage.at[me, pl.ds(0, 3)], r_out.at[pl.ds(0, 3), mine], lsem.at[6])
    qkv_own.start()

    relay(csend)
    weights_here((3,))

    def back(doc):
        got = lax.dot_general(cot[doc], wov[...], NT, preferred_element_type=F32).astype(BF)
        stage[2 * doc, 3] = got[:, :HDIM]
        stage[2 * doc + 1, 3] = got[:, HDIM:]
        for h in (0, 1):
            j = 2 * doc + h
            where = device(x, lax.div(j, 4) * 2 + p, lax.rem(j, 4), c)

            @pl.when(j != me)
            def _():
                remote(stage.at[j, 3], r_out.at[3, mine], bssem.at[j], brsem.at[me], where).start()

            @pl.when(j == me)
            def _():
                pltpu.make_async_copy(stage.at[j, 3], r_out.at[3, mine], lsem.at[7]).start()

    csend[2].wait_recv()
    back(x)
    csend[5].wait_recv()
    back(xl)
    csend[6].wait_recv()
    back(xr)
    csend[3].wait_recv()
    csend[7].start()
    csend[4].wait_recv()
    csend[8].start()
    csend[7].wait_recv()
    csend[8].wait_recv()
    back(x2)
    out_c = pltpu.make_async_copy(cot, cot_out, osem.at[1])
    out_c.start()
    for cp in tsend + csend + wsend:
        cp.wait_send()
    for cp in qkv:
        cp.wait()
    qkv_own.wait()
    for j in range(8):

        @pl.when(j != me)
        def _():
            cp = remote(stage.at[j, 3], r_out.at[3, pl.ds(j * CHIP_ROWS, CHIP_ROWS)], bssem.at[j], brsem.at[j], sib)
            cp.wait_send()
            cp.wait_recv()

    pltpu.make_async_copy(stage.at[me, 3], r_out.at[3, mine], lsem.at[7]).wait()
    out_t.wait()
    out_w.wait()
    out_c.wait()


def gather(tokens, cotangent, wq, wk, wv, wo):
    dma = pltpu.SemaphoreType.DMA
    return pl.pallas_call(
        gather_kernel,
        out_shape=(
            jax.ShapeDtypeStruct((4, CHIP_ROWS, D), BF),
            jax.ShapeDtypeStruct((4, CHIP_ROWS, D), BF),
            jax.ShapeDtypeStruct((3, D, 256), BF),
            jax.ShapeDtypeStruct((4, 2048, HDIM), BF),
        ),
        in_specs=[ANY] * 6,
        out_specs=(ANY,) * 4,
        scratch_shapes=[
            pltpu.VMEM((4, CHIP_ROWS, D), BF),
            pltpu.VMEM((4, CHIP_ROWS, D), BF),
            pltpu.VMEM((3, D, 256), BF),
            pltpu.VMEM((256, D), BF),
            pltpu.VMEM((8, 4, CHIP_ROWS, HDIM), BF),
            dma((2, 9)), dma((2, 9)), dma((4,)), dma((4, 2)), dma((8,)),
            dma((7,)), dma((7,)), dma((8,)), dma((8,)), dma((3,)),
        ],
        compiler_params=pltpu.CompilerParams(
            collective_id=0, has_side_effects=True, vmem_limit_bytes=44 << 20
        ),
        cost_estimate=pl.CostEstimate(flops=9 * 10**9, bytes_accessed=60 << 20, transcendentals=0),
    )(tokens, cotangent, wq, wk, wv, wo)


def attention_kernel(flags, pos_row, pos_col, r, o, kp, vp, dkp, dvp, kg, vg, dkg, dvg):
    n = 2048
    scale = HDIM**-0.5
    for dst, t in ((kp, 1), (vp, 2)):
        dst[:BLOCK] = jnp.zeros((BLOCK, HDIM), BF)
        dst[BLOCK : BLOCK + n] = r[t]
        dst[BLOCK + n :] = jnp.zeros((BLOCK, HDIM), BF)
    dkp[...] = jnp.zeros_like(dkp)
    dvp[...] = jnp.zeros_like(dvp)
    dkg[...] = jnp.zeros_like(dkg)
    dvg[...] = jnp.zeros_like(dvg)
    pick = (pos_col[...] == lax.broadcasted_iota(jnp.int32, (128, n), 1)).astype(F32).astype(BF)
    kg[...] = jnp.dot(pick, r[1], preferred_element_type=F32).astype(BF)
    vg[...] = jnp.dot(pick, r[2], preferred_element_type=F32).astype(BF)
    col = lax.div(lax.broadcasted_iota(jnp.int32, (1, 256), 1), 64)
    low = lax.broadcasted_iota(jnp.int32, (128, 256), 0) < BLOCK

    def nt(a, b):
        return lax.dot_general(a, b, NT, preferred_element_type=F32)

    def tn(a, b):
        return lax.dot_general(a, b, TN, preferred_element_type=F32)

    def step(i, _):
        rows = pl.ds(al(i * 128, 128), 128)
        win = pl.ds(al(i * 128, 128), 256)
        q, do = r[0, rows], r[3, rows]
        k, v = kp[win], vp[win]
        prev0 = jnp.where(i > 0, flags[4 * i], 0)
        next0 = flags[4 * i + 1]
        prev1 = flags[4 * i + 2]
        next1 = jnp.where(i < 15, flags[4 * i + 3], 0)
        m0 = jnp.where(col == 0, prev0, jnp.where(col == 1, 1, jnp.where(col == 2, next0, 0)))
        m1 = jnp.where(col == 0, 0, jnp.where(col == 1, prev1, jnp.where(col == 2, 1, next1)))
        seen = jnp.where(low, m0, m1) == 1
        sl = jnp.where(seen, nt(q, k) * scale, -jnp.inf)
        sg = nt(q, kg[...]) * scale
        top = jnp.maximum(sl.max(-1, keepdims=True), sg.max(-1, keepdims=True))
        el, eg = jnp.exp(sl - top), jnp.exp(sg - top)
        inv = 1.0 / (el.sum(-1, keepdims=True) + eg.sum(-1, keepdims=True))
        pl_, pg = el * inv, eg * inv
        plb, pgb = pl_.astype(BF), pg.astype(BF)
        ctx = jnp.dot(plb, v, preferred_element_type=F32) + jnp.dot(pgb, vg[...], preferred_element_type=F32)
        o[3, rows] = ctx.astype(BF)
        dl, dg = nt(do, v), nt(do, vg[...])
        delta = (pl_ * dl).sum(-1, keepdims=True) + (pg * dg).sum(-1, keepdims=True)
        zl = (pl_ * (dl - delta) * scale).astype(BF)
        zg = (pg * (dg - delta) * scale).astype(BF)
        gq = jnp.dot(zl, k, preferred_element_type=F32) + jnp.dot(zg, kg[...], preferred_element_type=F32)
        o[0, rows] = gq.astype(BF)
        dkp[win] += tn(zl, q)
        dvp[win] += tn(plb, do)
        dkg[...] += tn(zg, q)
        dvg[...] += tn(pgb, do)
        return 0

    lax.fori_loop(0, 16, step, 0)

    def split(a):
        high = a.astype(BF)
        return high, (a - high.astype(F32)).astype(BF)

    kh, klo = split(dkg[...])
    vh, vlo = split(dvg[...])

    def finish(i, _):
        rows = pl.ds(al(i * 128, 128), 128)
        inner = pl.ds(al(i * 128 + BLOCK, 64), 128)
        put = (pos_row[...] == i * 128 + lax.broadcasted_iota(jnp.int32, (128, 128), 0)).astype(F32).astype(BF)

        def dot(b):
            return jnp.dot(put, b, preferred_element_type=F32)

        o[1, rows] = (dkp[inner] + dot(kh) + dot(klo)).astype(BF)
        o[2, rows] = (dvp[inner] + dot(vh) + dot(vlo)).astype(BF)
        return 0

    lax.fori_loop(0, 16, finish, 0)


def attention(flags, pos, r):
    vm = pl.BlockSpec(memory_space=pltpu.VMEM)
    return pl.pallas_call(
        attention_kernel,
        out_shape=jax.ShapeDtypeStruct((4, 2048, HDIM), BF),
        in_specs=[pl.BlockSpec(memory_space=pltpu.SMEM), vm, vm, vm],
        out_specs=vm,
        scratch_shapes=[
            pltpu.VMEM((2176, HDIM), BF), pltpu.VMEM((2176, HDIM), BF),
            pltpu.VMEM((2176, HDIM), F32), pltpu.VMEM((2176, HDIM), F32),
            pltpu.VMEM((128, HDIM), BF), pltpu.VMEM((128, HDIM), BF),
            pltpu.VMEM((128, HDIM), F32), pltpu.VMEM((128, HDIM), F32),
        ],
        compiler_params=pltpu.CompilerParams(vmem_limit_bytes=32 << 20),
        cost_estimate=pl.CostEstimate(flops=2 * 10**9, bytes_accessed=4 << 20, transcendentals=10**6),
    )(flags, pos.reshape(1, 128), pos.reshape(128, 1), r)


def scatter_kernel(
    o_in, tok, cot, w_in,
    gt_out, wg_out,
    w, g, gt, part, pr, xa, xf, wp, za, zf, tb, cb, ya, yf, fs, gto,
    lsem, assem, arsem, sssem, srsem, xssem, xrsem, zssem, zrsem, yssem, yrsem, tsem, csem,
):
    x, y, z, c = place()
    p, yh = lax.rem(y, 2), lax.div(y, 2)
    xr, xl, x2 = mod4(x + 1), mod4(x - 1), mod4(x + 2)
    zr, zl, z2 = mod4(z + 1), mod4(z - 1), mod4(z + 2)
    right, left = device(xr, y, z, c), device(xl, y, z, c)
    front, rear = device(x, y, zr, c), device(x, y, zl, c)
    up, down = mod4(y + 1), mod4(y - 1)
    above, below = device(x, up, z, c), device(x, down, z, c)
    sib = device(x, y, z, 1 - c)
    me = yh * 4 + z
    peers = [chip_peer(x, y, z, c, k) for k in range(1, 8)]
    meet([right, left, sib, above, below] + [where for _, where in peers])

    def spot(j):
        return g.at[
            :, pl.ds(al(lax.div(j, 2) * CHIP_ROWS, CHIP_ROWS), CHIP_ROWS), pl.ds(al(lax.rem(j, 2) * HDIM, HDIM), HDIM)
        ]

    def rows_of(j):
        return o_in.at[:, pl.ds(al(j * CHIP_ROWS, CHIP_ROWS), CHIP_ROWS)]

    a2a = [
        remote(rows_of(j), spot(me), assem.at[k], arsem.at[k], where) for k, (j, where) in enumerate(peers)
    ]
    for cp in a2a:
        cp.start()
    own_part = pltpu.make_async_copy(rows_of(me), spot(me), lsem.at[0])
    own_part.start()
    w_load = pltpu.make_async_copy(w_in, w, lsem.at[1])

    groups = (z2, zr, zl, z)
    order = [(0, 0), (0, 1), (1, 1), (2, 0), (1, 0), (2, 1), (3, 0), (3, 1)]

    def load(n):
        o, ab = order[n]
        cols = pl.ds(al(ab * 2048 + groups[o] * 512, 512), 512)
        slot = n % 2
        return (
            pltpu.make_async_copy(tok.at[:, :, cols], tb.at[slot], tsem.at[slot]),
            pltpu.make_async_copy(cot.at[:, :, cols], cb.at[slot], csem.at[slot]),
        )

    def fetch(n):
        for cp in load(n):
            cp.start()

    fetch(0)
    w_load.start()
    for cp in a2a:
        cp.wait()
    own_part.wait()

    @pl.loop(0, 4)
    def _(t):
        for i in range(4):
            rows = pl.ds(i * 256, 256)
            gt[pl.ds(al(t * 256, 256), 256), rows] = g[t, rows].T

    def piece(n):
        o, ab = order[n]
        slot = n % 2
        if n + 1 < len(order):
            fetch(n + 1)
        for cp in load(n):
            cp.wait()

        def body(src):
            def run(i):
                rows = pl.ds(al(i * 256, 256), 256)
                acc = jnp.zeros((256, 512), F32)
                for b in range(4):
                    acc += jnp.dot(
                        gt[rows, pl.ds(b * 256, 256)], src[slot, b], preferred_element_type=F32
                    )
                wp[o, ab, rows] = acc.astype(BF)

            return run

        pl.loop(0, 3)(body(tb))
        body(cb)(3)

    docs = (x2, xr, xl, x)
    own = pl.ds(al(c * ROWS, ROWS), ROWS)
    other = pl.ds(al((1 - c) * ROWS, ROWS), ROWS)
    to_sib = [remote(part.at[o, other], pr.at[o], sssem.at[o], srsem.at[o], sib) for o in range(4)]

    def tokens_part(o):
        rows = pl.ds(al(docs[o] * CHIP_ROWS, CHIP_ROWS), CHIP_ROWS)

        @pl.loop(0, 8)
        def _(n):
            cols = pl.ds(al(n * 512, 512), 512)
            acc = jnp.zeros((CHIP_ROWS, 512), F32)
            for t in range(3):
                acc += lax.dot_general(g[t, rows], w[t, cols], NT, preferred_element_type=F32)
            part[o, :, cols] = acc.astype(BF)

        to_sib[o].start()

    def z_copy(i, src, dst, where):
        return remote(src, dst, zssem.at[i], zrsem.at[i], where)

    zc = [
        z_copy(0, wp.at[0, 0], za.at[0], front),
        z_copy(1, wp.at[0, 1], za.at[1], rear),
        z_copy(2, wp.at[1, 1], zf.at[0, 1], front),
        z_copy(3, wp.at[2, 0], zf.at[1, 0], rear),
        z_copy(4, wp.at[1, 0], zf.at[0, 0], front),
        z_copy(5, wp.at[2, 1], zf.at[1, 1], rear),
    ]
    xc = [
        remote(pr.at[0, pl.ds(0, 64)], xa.at[pl.ds(0, 64)], xssem.at[0], xrsem.at[0], right),
        remote(pr.at[0, pl.ds(64, 64)], xa.at[pl.ds(64, 64)], xssem.at[1], xrsem.at[1], left),
        remote(pr.at[1], xf.at[0], xssem.at[2], xrsem.at[2], right),
        remote(pr.at[2], xf.at[1], xssem.at[3], xrsem.at[3], left),
    ]

    piece(0)
    zc[0].start()
    piece(1)
    zc[1].start()
    w_load.wait()
    tokens_part(0)
    piece(2)
    zc[2].start()
    tokens_part(1)
    piece(3)
    zc[3].start()

    def sum_rows(o, extra=None):
        @pl.loop(0, 8)
        def _(n):
            cols = pl.ds(al(n * 512, 512), 512)
            for h in range(2):
                rows = pl.ds(h * 64, 64)
                mine = pl.ds(al(c * ROWS + h * 64, 64), 64)
                total = part[o, mine, cols].astype(F32) + pr[o, rows, cols].astype(F32)
                if extra is not None and extra == h:
                    total += xa[rows, cols].astype(F32)
                pr[o, rows, cols] = total.astype(BF)

    to_sib[0].wait_recv()
    sum_rows(0)
    xc[0].start()
    xc[1].start()
    tokens_part(2)
    tokens_part(3)
    piece(4)
    piece(5)
    piece(6)
    piece(7)
    to_sib[1].wait_recv()
    to_sib[2].wait_recv()
    to_sib[3].wait_recv()
    xc[0].wait_recv()
    sum_rows(1, 0)
    xc[2].start()
    xc[1].wait_recv()
    sum_rows(2, 1)
    xc[3].start()

    def add_piece(o, ab, src):
        @pl.loop(0, 16)
        def _(i):
            rows = pl.ds(al(i * 64, 64), 64)
            total = wp[o, ab, rows].astype(F32) + src[rows].astype(F32)
            wp[o, ab, rows] = total.astype(BF)

    zc[0].wait_recv()
    add_piece(1, 0, za.at[0])
    zc[4].start()
    zc[1].wait_recv()
    add_piece(2, 1, za.at[1])
    zc[5].start()

    xc[2].wait_recv()
    xc[3].wait_recv()

    @pl.loop(0, 8)
    def _(n):
        cols = pl.ds(al(n * 512, 512), 512)
        total = part[3, own, cols].astype(F32) + pr[3, :, cols].astype(F32)
        total += xf[0, :, cols].astype(F32) + xf[1, :, cols].astype(F32)
        gto[:, cols] = total.astype(BF)

    gt_copy = pltpu.make_async_copy(gto, gt_out, lsem.at[2])
    gt_copy.start()

    for i in (2, 3, 4, 5):
        zc[i].wait_recv()
    for ab in range(2):

        @pl.loop(0, 16)
        def _(i):
            rows = pl.ds(al(i * 64, 64), 64)
            total = wp[3, ab, rows].astype(F32) + zf[0, ab, rows].astype(F32) + zf[1, ab, rows].astype(F32)
            wp[3, ab, rows] = total.astype(BF)

    lo, hi = pl.ds(0, 512), pl.ds(512, 512)

    def y_copy(i, src, dst, where):
        return remote(src, dst, yssem.at[i], yrsem.at[i], where)

    give = [
        y_copy(0, wp.at[3, 1 - yh, lo], ya.at[0], above),
        y_copy(1, wp.at[3, 1 - yh, hi], ya.at[1], below),
    ]
    pass_on = [
        y_copy(2, wp.at[3, lax.div(up, 2)], yf.at[0], above),
        y_copy(3, wp.at[3, lax.div(down, 2)], yf.at[1], below),
    ]
    final = remote(fs.at[1], wg_out, yssem.at[4], yrsem.at[4], sib)
    final_own = pltpu.make_async_copy(fs.at[0], wg_out, lsem.at[3])

    @pl.when(c == p)
    def _():
        for cp in give:
            cp.start()
        for cp in pass_on:
            cp.wait_recv()

        @pl.loop(0, 16)
        def _(i):
            rows = pl.ds(al(i * 64, 64), 64)

            def total(cols):
                return (
                    wp[3, yh, rows, cols].astype(F32) + yf[0, rows, cols].astype(F32) + yf[1, rows, cols].astype(F32)
                )

            fs[0, rows] = total(pl.ds(al(c * 256, 256), 256))
            fs[1, rows] = total(pl.ds(al((1 - c) * 256, 256), 256))

        final.start()
        final_own.start()
        for cp in give:
            cp.wait_send()
        final.wait_send()
        final_own.wait()

    @pl.when(c != p)
    def _():
        for i, cp in enumerate(give):
            cp.wait_recv()
            idx = lax.div((up, down)[i], 2)

            @pl.loop(0, 8)
            def _(n):
                part_rows = pl.ds(al(n * 64, 64), 64)
                rows = pl.ds(al(i * 512 + n * 64, 64), 64)
                total = wp[3, idx, rows].astype(F32) + ya[i, part_rows].astype(F32)
                wp[3, idx, rows] = total.astype(BF)

            pass_on[i].start()
        for cp in pass_on:
            cp.wait_send()
        final.wait_recv()

    for cp in to_sib + xc + zc:
        cp.wait_send()
    gt_copy.wait()


def scatter(o, tok, cot, w):
    dma = pltpu.SemaphoreType.DMA
    vm = pltpu.VMEM
    return pl.pallas_call(
        scatter_kernel,
        out_shape=(jax.ShapeDtypeStruct((ROWS, D), BF), jax.ShapeDtypeStruct((1024, 256), F32)),
        in_specs=[ANY] * 4,
        out_specs=(ANY,) * 2,
        scratch_shapes=[
            vm((3, D, 256), BF),
            vm((4, 1024, 256), BF),
            vm((1024, 1024), BF),
            vm((4, CHIP_ROWS, D), BF),
            vm((4, ROWS, D), BF),
            vm((ROWS, D), BF),
            vm((2, ROWS, D), BF),
            vm((4, 2, 1024, 512), BF),
            vm((2, 1024, 512), BF),
            vm((2, 2, 1024, 512), BF),
            vm((2, 4, CHIP_ROWS, 512), BF),
            vm((2, 4, CHIP_ROWS, 512), BF),
            vm((2, 512, 512), BF),
            vm((2, 1024, 512), BF),
            vm((2, 1024, 256), F32),
            vm((ROWS, D), BF),
            dma((4,)), dma((7,)), dma((7,)), dma((4,)), dma((4,)), dma((4,)), dma((4,)),
            dma((6,)), dma((6,)), dma((5,)), dma((5,)), dma((2,)), dma((2,)),
        ],
        compiler_params=pltpu.CompilerParams(
            collective_id=1, has_side_effects=True, vmem_limit_bytes=58 << 20
        ),
        cost_estimate=pl.CostEstimate(flops=15 * 10**9, bytes_accessed=60 << 20, transcendentals=0),
    )(o, tok, cot, w)


def on_device(tokens, cotangent, w_query, w_key, w_value, w_output, global_pos, pattern):
    flags = lax.all_gather(pattern, "seq", axis=1, tiled=True)
    tok, cot, w, r = gather(tokens[0], cotangent[0], w_query, w_key, w_value, w_output)
    x, y, z, c = place()
    doc = lax.div(lax.div(y, 2) * 4 + z, 2) * 2 + lax.rem(y, 2)
    pos = lax.dynamic_index_in_dim(global_pos, doc, 0, keepdims=False)
    flag = lax.dynamic_index_in_dim(flags, doc, 0, keepdims=False).reshape(-1)
    o = attention(flag, pos, r)
    grad_tokens, grads = scatter(o, tok, cot, w)
    return (
        grad_tokens[None],
        grads[:256].T,
        grads[256:512].T,
        grads[512:768].T,
        grads[768:],
    )


def solution(mesh):
    in_specs = (
        P("fsdp", "seq", None),
        P("fsdp", "seq", None),
        P(None, "fsdp"),
        P(None, "fsdp"),
        P(None, "fsdp"),
        P("fsdp", None),
        P(),
        P(None, "seq", None),
    )
    out_specs = (
        P("fsdp", "seq", None),
        P("seq", "fsdp"),
        P("seq", "fsdp"),
        P("seq", "fsdp"),
        P("fsdp", "seq"),
    )
    return jax.shard_map(
        on_device, mesh=mesh, in_specs=in_specs, out_specs=out_specs, check_vma=False
    )
```

time: 1010 us -> 282 us (0.28)
  waiting for transfers between devices: 820 us -> 0 us
  Pallas kernels: 0 us -> 239 us
  matrix products: 99.9 us -> 0 us
  blocking collectives: 0 us -> 27.2 us
  local copies, waits for them, and re-layouts: 40.9 us -> 14.1 us
  other arithmetic: 16.4 us -> 0 us
  between operations: 15 us -> 0.74 us
  starting transfers between devices: 12.5 us -> 0 us
    all_gather x2 -> x0, waiting for transfers between devices: 322 us -> none  [the longest x1 172 us: on_device(): inputs = lax.all_gather(tokens, 'fsdp', axis=0, tiled=True)]
    psum x2 -> x0, waiting for transfers between devices: 257 us -> none  [the longest x1 141 us: on_device(): global_kv = lax.psum(picked.astype(jnp.bfloat16), 'seq')]
    pallas_call x0 -> x3, Pallas kernels: none -> 239 us  [the longest x1 140 us: scatter(): pl.pallas_call(scatter_kernel, out_shape=(jax.ShapeDtypeStruct((ROWS, D),...]
    reduce_scatter x2 -> x0, waiting for transfers between devices: 232 us -> none  [the longest x1 168 us: on_device(): lax.psum_scatter(partial_value.astype(jnp.bfloat16), 'fsdp', scatter_dime...]
    dot_general x23 -> x0, matrix products: 98.9 us -> none  [the longest x4 43.5 us: contract_cols(): lax.dot_general(left, right, (((1,), (1,)), ((), ())), preferred_element_...]
    all_gather x0 -> x1, blocking collectives: none -> 27.2 us  [on_device(): flags = lax.all_gather(pattern, 'seq', axis=1, tiled=True)]
    ppermute x4 -> x0, starting transfers between devices: 11.4 us -> none  [the longest x2 6.03 us: with_halo(): before = lax.ppermute(last, axis, up)]
  transfers between devices with their start and end apart: 10 -> 0, of which waited for: 8 -> 0; matrix products, arithmetic and copies ran while one was open for 10% -> 0% of each run, Pallas kernels for 0% -> 0%
where the time goes in v1:
time: 282 us; the launch traced here: 281 us
  Pallas kernels  239 us (85%)
  blocking collectives  27.2 us (10%)
  local copies, waits for them, and re-layouts  14.1 us (5%)
    pallas_call x1, Pallas kernels, scatter(): pl.pallas_call(scatter_kernel, out_shape=(jax.ShapeDtypeStruct((ROWS, D),...  140 us
    pallas_call x1, Pallas kernels, gather(): pl.pallas_call(gather_kernel, out_shape=(jax.ShapeDtypeStruct((4, CHIP_RO...  81.7 us
    all_gather x1, blocking collectives, on_device(): flags = lax.all_gather(pattern, 'seq', axis=1, tiled=True)  27.2 us
    pallas_call x1, Pallas kernels, attention(): pl.pallas_call(attention_kernel, out_shape=jax.ShapeDtypeStruct((4, 2048,...  17.6 us
    unnamed x18, local copies, waits for them, and re-layouts  11.1 us

profile of v1, /device:TPU:1, one launch (start us, length us, event | category | flops | bytes accessed | tf_op | source)
XLA Modules:
  0.0 281.3 jit_solution(10752587967114061189)
XLA Ops:
  0.6 0.0 copy-start
  0.7 0.6 copy-done
  1.3 27.2 %all_gather.3 = s32[8,32,2]{0,2,1:T(2,128)S(1)} all-gather(s32[8,2,2]{0,2,1:T(2,128)} %param.15), channel_id=1, replica_groups=mesh['seq'=16,'fsdp'=8] {'seq'}, dimensions={1}, use_global_device_ids=true | all-gather | bytes 2176 | tf_op jit(solution)/shard_map/all_gather | solution.py:670
  28.6 0.7 dynamic-slice_reduce_fusion
  29.3 0.1 reshape.19.flags
  29.4 0.1 copy.21.pos_col
  29.5 0.0 copy-start.1
  29.5 1.6 copy-done.1
  31.1 0.0 copy-start.2
  31.1 1.6 copy-done.2
  32.7 1.2 copy-done.3
  33.9 1.2 copy-done.4
  35.1 81.7 %shard_map.119 = (bf16[4,256,4096]{2,1,0:T(8,128)(2,1)}, bf16[4,256,4096]{2,1,0:T(8,128)(2,1)}, bf16[3,4096,256]{2,1,0:T(8,128)(2,1)}, bf16[4,2048,128]{2,1,0:T(8,128)(2,1)S(1)}) custom-call(bf16[128,4096]{1,0:T(8,128)(2,1)S(1)} %bitcast.11, bf16[128,4096]{1,0:T(8,128)(2,1)S(1)} %bitcast.12, bf16[4096,256]{1,0:T(8,128)(2,1)S(1)} %copy-done.1, ...), custom_call_target="tpu_custom_call" | custom-call | flops 8999999488 | bytes 62914560 | tf_op jit(solution)/shard_map/pallas_call | solution.py:241
  116.9 17.6 %shard_map.120.o_in = bf16[4,2048,128]{2,1,0:T(8,128)(2,1)S(1)} custom-call(s32[64]{0:T(128)S(1)} %reshape.19.flags, s32[1,128]{1,0:T(1,128)S(1)} %constant_dynamic-slice_fusion.pos_row, s32[128,1]{1,0:T(8,128)S(1)} %copy.21.pos_col, bf16[4,2048,128]{2,1,0:T(8,128)(2,1)S(1)} %get-tuple-element.11.r), custom_call_target="tpu_custom_call" | custom-call | flops 2000000000 | bytes 4194304 | tf_op jit(solution)/shard_map/pallas_call | solution.py:349
  134.4 0.0 copy-start.5
  134.4 1.3 copy-done.5
  135.8 139.9 %shard_map.121 = (bf16[128,4096]{1,0:T(8,128)(2,1)}, f32[1024,256]{1,0:T(8,128)}) custom-call(bf16[4,2048,128]{2,1,0:T(8,128)(2,1)} %copy-done.5, bf16[4,256,4096]{2,1,0:T(8,128)(2,1)} %get-tuple-element.12.tok, bf16[4,256,4096]{2,1,0:T(8,128)(2,1)} %get-tuple-element.13.cot, bf16[3,4096,256]{2,1,0:T(8,128)(2,1)} %get-tuple-element.14.w_in), custom_call_target="tpu_custom_call" | custom-call | flops 15000000512 | bytes 62914560 | tf_op jit(solution)/shard_map/pallas_call | solution.py:637
  275.7 0.0 copy-start.6
  275.7 2.0 fusion
  277.8 0.8 copy.24
  278.6 0.8 copy.23
  279.5 0.8 copy.22
  280.3 0.0 copy-done.6
  280.3 1.0 copy.26
  (4 shorter events, 0.0 us)
Async XLA Ops:
  0.6 0.7 copy-start
  29.5 1.6 copy-start.1
  31.1 1.6 copy-start.2
  32.7 1.2 copy-start.3
  33.9 1.2 copy-start.4
  134.4 1.4 copy-start.5
  275.7 4.6 %copy-start.6 = (bf16[128,4096]{1,0:T(8,128)(2,1)S(1)}, bf16[128,4096]{1,0:T(8,128)(2,1)}, u32[]{:S(2)}) copy-start(bf16[128,4096]{1,0:T(8,128)(2,1)} %get-tuple-element.15) | copy-start | bytes 3145732

commit v2 on v1

v2 whole, which is shorter than its diff:
```python
import jax
import jax.numpy as jnp
from jax import lax
from jax.experimental import pallas as pl
from jax.experimental.pallas import tpu as pltpu
from jax.sharding import PartitionSpec as P

BLOCK = 64
HDIM = 128
ROWS = 128
CHIP_ROWS = 256
D = 4096
BF = jnp.bfloat16
F32 = jnp.float32
MESH = pl.DeviceIdType.MESH
ANY = pl.BlockSpec(memory_space=pl.ANY)
NT = (((1,), (1,)), ((), ()))
TN = (((0,), (0,)), ((), ()))


def place():
    f = lax.axis_index("fsdp")
    s = lax.axis_index("seq")
    x, p = lax.div(f, 2), lax.rem(f, 2)
    yh, z, c = lax.div(s, 8), lax.rem(lax.div(s, 2), 4), lax.rem(s, 2)
    return x, 2 * yh + p, z, c


def device(x, y, z, c):
    return {"seq": lax.div(y, 2) * 8 + z * 2 + c, "fsdp": x * 2 + lax.rem(y, 2)}


def mod4(v):
    return lax.rem(v + 4, 4)


def al(v, n):
    return pl.multiple_of(v, n)


def remote(src, dst, send, recv, where):
    return pltpu.make_async_remote_copy(
        src_ref=src, dst_ref=dst, send_sem=send, recv_sem=recv, device_id=where, device_id_type=MESH
    )


def meet(devices):
    barrier = pltpu.get_barrier_semaphore()
    for where in devices:
        pl.semaphore_signal(barrier, inc=1, device_id=where, device_id_type=MESH)
    pl.semaphore_wait(barrier, len(devices))


def chip_peer(x, y, z, c, k):
    j = lax.rem(lax.div(y, 2) * 4 + z + k, 8)
    return j, device(x, lax.div(j, 4) * 2 + lax.rem(y, 2), lax.rem(j, 4), c)


HALF_Q, HALF_O = 384, 128


class Reduce:
    def __init__(self, at, rows, bufs, sems):
        self.at, self.rows = at, rows
        self.wz, self.za, self.zf, self.yf, self.wy, self.yg, self.zb, self.zg = bufs
        ss, rs = sems
        half = rows // 2
        lo, hi = pl.ds(0, half), pl.ds(half, half)
        self.lo, self.hi = lo, hi
        wz, za, zf, yf, wy, yg, zb, zg = bufs
        up, down, yh = at["up"], at["down"], at["yh"]
        front, rear, above, below = at["front"], at["rear"], at["above"], at["below"]
        up_i, down_i = lax.div(up, 2), lax.div(down, 2)
        self.up_i, self.down_i, self.yh = up_i, down_i, yh

        def cp(i, src, dst, where):
            return remote(src, dst, ss.at[i], rs.at[i], where)

        self.z = [
            cp(0, wz.at[0, 0], za.at[0], front),
            cp(1, wz.at[0, 1], za.at[1], rear),
            cp(2, wz.at[1, 1], zf.at[0, 1], front),
            cp(3, wz.at[2, 0], zf.at[1, 0], rear),
            cp(4, wz.at[1, 0], zf.at[0, 0], front),
            cp(5, wz.at[2, 1], zf.at[1, 1], rear),
        ]
        self.give = [
            cp(6, wy.at[1 - yh, :, lo], yg.at[0, :, lo], above),
            cp(7, wy.at[1 - yh, :, hi], yg.at[1, :, lo], below),
        ]
        self.free = [
            cp(8, wy.at[up_i, :, hi], yg.at[0, :, hi], above),
            cp(9, wy.at[down_i, :, lo], yg.at[1, :, lo], below),
        ]
        self.dep = [
            cp(6, wy.at[up_i, :, lo], yg.at[0, :, lo], above),
            cp(7, wy.at[down_i, :, hi], yg.at[1, :, hi], below),
        ]
        self.zy_give = [
            cp(10, wz.at[3, 1 - yh, lo], yf.at[0, lo], above),
            cp(11, wz.at[3, 1 - yh, hi], yf.at[1, lo], below),
        ]
        self.zy_pass = [
            cp(12, wz.at[3, up_i], yf.at[0], above),
            cp(13, wz.at[3, down_i], yf.at[1], below),
        ]
        self.yz = [
            cp(14, wy.at[yh, 0, lo], zb.at[0], front),
            cp(15, wy.at[yh, 0, hi], zb.at[1], rear),
            cp(16, wy.at[yh, 1], zg.at[0], front),
            cp(17, wy.at[yh, 2], zg.at[1], rear),
        ]

    def add(self, rows, dst, *srcs):
        @pl.loop(0, rows // 64)
        def _(i):
            r = pl.ds(al(i * 64, 64), 64)
            total = dst[r].astype(F32)
            for s in srcs:
                total += s[r].astype(F32)
            dst[r] = total.astype(BF)

    def start_y(self):
        @pl.when(self.at["owner"])
        def _():
            for cp in self.give:
                cp.start()

        @pl.when(self.at["middle"])
        def _():
            for cp in self.free:
                cp.start()

    def dep_z(self):
        self.z[0].wait_recv()
        self.add(self.rows, self.wz.at[1, 0], self.za.at[0])
        self.z[4].start()
        self.z[1].wait_recv()
        self.add(self.rows, self.wz.at[2, 1], self.za.at[1])
        self.z[5].start()

    def dep_y(self):
        half = self.rows // 2

        @pl.when(self.at["middle"])
        def _():
            for i, (idx, part) in enumerate(((self.up_i, self.lo), (self.down_i, self.hi))):
                self.give[i].wait_recv()
                for o in range(4):
                    self.add(half, self.wy.at[idx, o, part], self.yg.at[i, o, self.lo])
                self.dep[i].start()

    def mid_z(self):
        for i in (2, 3, 4, 5):
            self.z[i].wait_recv()
        for ab in range(2):
            self.add(self.rows, self.wz.at[3, ab], self.zf.at[0, ab], self.zf.at[1, ab])

        @pl.when(self.at["owner"])
        def _():
            for cp in self.zy_give:
                cp.start()

    def mid_y(self):
        @pl.when(self.at["owner"])
        def _():
            for cp in self.free + self.dep:
                cp.wait_recv()
            for cp in self.give:
                cp.wait_send()
            for o in range(4):
                self.add(self.rows, self.wy.at[self.yh, o], self.yg.at[0, o], self.yg.at[1, o])
                if o == 0:
                    self.yz[0].start()
                    self.yz[1].start()

    def last_z(self):
        half = self.rows // 2

        @pl.when(self.at["middle"])
        def _():
            for i, (idx, part) in enumerate(((self.up_i, self.lo), (self.down_i, self.hi))):
                self.zy_give[i].wait_recv()
                self.add(half, self.wz.at[3, idx, part], self.yf.at[i, self.lo])
                self.zy_pass[i].start()

    def last_y(self):
        half = self.rows // 2

        @pl.when(self.at["owner"])
        def _():
            self.yz[0].wait_recv()
            self.add(half, self.wy.at[self.yh, 1, self.lo], self.zb.at[0])
            self.yz[2].start()
            self.yz[1].wait_recv()
            self.add(half, self.wy.at[self.yh, 2, self.hi], self.zb.at[1])
            self.yz[3].start()

    def result(self, put):
        for cp in self.zy_pass:
            cp.wait_recv()
        for n in range(self.rows // 128):
            rows = pl.ds(n * 128, 128)
            put(0, n, lambda cols: (
                self.wz[3, self.yh, rows, cols].astype(F32)
                + self.yf[0, rows, cols].astype(F32) + self.yf[1, rows, cols].astype(F32)))
        for cp in self.yz[2:]:
            cp.wait_recv()
        for n in range(self.rows // 128):
            rows = pl.ds(n * 128, 128)
            put(1, n, lambda cols: (
                self.wy[self.yh, 3, rows, cols].astype(F32)
                + self.zg[0, rows, cols].astype(F32) + self.zg[1, rows, cols].astype(F32)))

    def drain(self):
        for cp in self.z:
            cp.wait_send()

        @pl.when(self.at["owner"])
        def _():
            for cp in self.zy_give + self.yz:
                cp.wait_send()

        @pl.when(self.at["middle"])
        def _():
            for cp in self.free + self.dep + self.zy_pass:
                cp.wait_send()


def reduce_scratch(rows):
    vm = pltpu.VMEM
    return [
        vm((4, 2, rows, 512), BF), vm((2, rows, 512), BF), vm((2, 2, rows, 512), BF), vm((2, rows, 512), BF),
        vm((2, 4, rows, 512), BF), vm((2, 4, rows, 512), BF), vm((2, rows // 2, 512), BF), vm((2, rows, 512), BF),
        pltpu.SemaphoreType.DMA((18,)), pltpu.SemaphoreType.DMA((18,)),
    ]


def kernel(
    pat, gpos, tok_in, cot_in, wq, wk, wv, wo,
    gt_out, gq_out, gk_out, gv_out, go_out,
    tok, cot, w, wov, r, g, gt, mask, masks, kg, vg, dkg, dvg, dkp, dvp, pr, xa, xf, fs,
    *rest,
):
    o_bufs, o_sems, q_bufs, q_sems = rest[:8], rest[8:10], rest[10:18], rest[18:20]
    (ssem, rsem, wssem, wrsem, lsem, mssem, mrsem, assem, arsem, bssem, brsem,
     cssem, crsem, dssem, drsem, essem, ersem, sssem, srsem, xssem, xrsem, fssem, frsem, flsem) = rest[20:]
    x, y, z, c = place()
    p, yh = lax.rem(y, 2), lax.div(y, 2)
    seq = lax.axis_index("seq")
    xr, xl, x2 = mod4(x + 1), mod4(x - 1), mod4(x + 2)
    zr, zl, z2 = mod4(z + 1), mod4(z - 1), mod4(z + 2)
    up, down = mod4(y + 1), mod4(y - 1)
    right, left = device(xr, y, z, c), device(xl, y, z, c)
    sib = device(x, y, z, 1 - c)
    me = yh * 4 + z
    my_doc = lax.div(me, 2) * 2 + p
    peers = [chip_peer(x, y, z, c, k) for k in range(1, 8)]

    kb = lax.div(lax.broadcasted_iota(jnp.int32, (8, 256), 1), 64)
    upper = lax.broadcasted_iota(jnp.int32, (8, 256), 0) == 0

    @pl.loop(0, 8)
    def _(d):
        prev0 = jnp.where(seq > 0, pat[d, 0, 0], 0)
        next0, prev1 = pat[d, 0, 1], pat[d, 1, 0]
        next1 = jnp.where(seq < 15, pat[d, 1, 1], 0)
        m0 = jnp.where(kb == 0, prev0, jnp.where(kb == 1, 1, jnp.where(kb == 2, next0, 0)))
        m1 = jnp.where(kb == 0, 0, jnp.where(kb == 1, prev1, jnp.where(kb == 2, 1, next1)))
        mask[c, d] = jnp.where(jnp.where(upper, m0, m1) == 1, 0.0, -jnp.inf)

    for t in (1, 2):
        r[t, :BLOCK] = jnp.zeros((BLOCK, HDIM), BF)
        r[t, BLOCK + 2048 :] = jnp.zeros((BLOCK, HDIM), BF)

    meet(
        [right, left, sib]
        + [device(x, v, z, core) for v in (up, down) for core in (0, 1)]
        + [where for _, where in peers]
    )
    own = pl.ds(al(c * ROWS, ROWS), ROWS)
    other = pl.ds(al((1 - c) * ROWS, ROWS), ROWS)
    first = pl.ds(al(c * ROWS, 64), 64)
    second = pl.ds(al(c * ROWS + 64, 64), 64)

    def sends(a, given, buf):
        def cp(kind, src, dst, where):
            return remote(src, dst, ssem.at[a, kind], rsem.at[a, kind], where)

        return [
            cp(0, given, buf.at[x, own], right),
            cp(1, given, buf.at[x, own], left),
            cp(2, given, buf.at[x, own], sib),
            cp(3, buf.at[xl, first], buf.at[xl, first], right),
            cp(4, buf.at[xr, second], buf.at[xr, second], left),
            cp(5, buf.at[xl, own], buf.at[xl, own], sib),
            cp(6, buf.at[xr, own], buf.at[xr, own], sib),
            cp(7, buf.at[x2, first], buf.at[x2, first], sib),
            cp(8, buf.at[x2, second], buf.at[x2, second], sib),
        ]

    tsend = sends(0, tok_in, tok)
    csend = sends(1, cot_in, cot)
    wdev = device(x, mod4(y + 1 + 2 * c), z, p)
    half = pl.ds(al(c * 2048, 2048), 2048)
    half_o = pl.ds(al(c * 128, 128), 128)
    wsend = [
        remote(src.at[half], w.at[t, half], wssem.at[t], wrsem.at[t, c], wdev)
        for t, src in enumerate((wq, wk, wv))
    ]
    wsend.append(remote(wo.at[half_o], wov.at[half_o], wssem.at[3], wrsem.at[3, c], wdev))
    wlocal = [pltpu.make_async_copy(src, w.at[t], lsem.at[t]) for t, src in enumerate((wq, wk, wv))]
    wlocal.append(pltpu.make_async_copy(wo, wov, lsem.at[3]))
    tlocal = pltpu.make_async_copy(tok_in, tok.at[x, own], lsem.at[4])
    clocal = pltpu.make_async_copy(cot_in, cot.at[x, own], lsem.at[5])

    for k in (0, 1, 2):
        tsend[k].start()
    for cp in wsend:
        cp.start()
    tlocal.start()
    clocal.start()

    @pl.when(c == p)
    def _():
        for cp in wlocal:
            cp.start()

    mask_sib = remote(mask.at[c], mask.at[c], mssem.at[7], mrsem.at[7], sib)
    mask_sib.start()
    mask_sib.wait()
    mask_out = [
        remote(mask.at[:, lax.div(j, 2) * 2 + p], masks.at[me], mssem.at[k], mrsem.at[k], where)
        for k, (j, where) in enumerate(peers)
    ]
    for cp in mask_out:
        cp.start()
    mask_own = pltpu.make_async_copy(mask.at[:, my_doc], masks.at[me], lsem.at[8])
    mask_own.start()

    def relay(copies):
        copies[0].wait_recv()
        copies[3].start()
        copies[5].start()
        copies[1].wait_recv()
        copies[4].start()
        copies[6].start()

    relay(tsend)
    for k in (0, 1, 2):
        csend[k].start()
    tsend[3].wait_recv()
    tsend[7].start()
    tsend[4].wait_recv()
    tsend[8].start()
    tlocal.wait()
    clocal.wait()

    def weights_here(ts):
        @pl.when(c == p)
        def _():
            for t in ts:
                wlocal[t].wait()

        @pl.when(c != p)
        def _():
            for t in ts:
                for h in (0, 1):
                    if t < 3:
                        ref = w.at[t, pl.ds(h * 2048, 2048)]
                    else:
                        ref = wov.at[pl.ds(h * 128, 128)]
                    remote(ref, ref, wssem.at[t], wrsem.at[t, h], sib).wait_recv()

    weights_here((0, 1, 2))
    for k in (2, 5, 6, 7, 8):
        tsend[k].wait_recv()

    def box(j, t):
        return gt.at[t, :, pl.ds(al(j * HDIM, HDIM), HDIM)]

    @pl.loop(0, 4)
    def _(doc):
        @pl.loop(0, 3)
        def _(t):
            got = jnp.dot(tok[doc], w[t], preferred_element_type=F32).astype(BF)
            gt[t, :, pl.ds(al(doc * 256, 256), 256)] = got

    mine = pl.ds(al(me * CHIP_ROWS + BLOCK, 64), CHIP_ROWS)

    def boxes(j, t0, n):
        return gt.at[pl.ds(t0, n), :, pl.ds(al(j * HDIM, HDIM), HDIM)]

    qkv = [
        remote(boxes(j, 0, 3), r.at[pl.ds(0, 3), mine], assem.at[k], arsem.at[k], where)
        for k, (j, where) in enumerate(peers)
    ]
    for cp in qkv:
        cp.start()
    qkv_own = pltpu.make_async_copy(boxes(me, 0, 3), r.at[pl.ds(0, 3), mine], lsem.at[6])
    qkv_own.start()

    relay(csend)
    weights_here((3,))

    def back(doc):
        got = lax.dot_general(cot[doc], wov[...], NT, preferred_element_type=F32).astype(BF)
        gt[3, :, pl.ds(al(doc * 256, 256), 256)] = got
        for h in (0, 1):
            j = 2 * doc + h
            where = device(x, lax.div(j, 4) * 2 + p, lax.rem(j, 4), c)

            @pl.when(j != me)
            def _():
                remote(box(j, 3), r.at[3, mine], bssem.at[j], brsem.at[me], where).start()

            @pl.when(j == me)
            def _():
                pltpu.make_async_copy(box(j, 3), r.at[3, mine], lsem.at[7]).start()

    csend[2].wait_recv()
    back(x)

    for cp in qkv:
        cp.wait()
    qkv_own.wait()
    for cp in mask_out:
        cp.wait()
    mask_own.wait()
    scale = HDIM**-0.5
    pos = jnp.broadcast_to(gpos[pl.ds(my_doc, 1), :], (128, 128))
    pos_t = pos.T
    lane = lax.broadcasted_iota(jnp.int32, (128, 128), 1)
    sub = lax.broadcasted_iota(jnp.int32, (128, 128), 0)
    low = lax.broadcasted_iota(jnp.int32, (128, 256), 0) < BLOCK

    def nt(a, b):
        return lax.dot_general(a, b, NT, preferred_element_type=F32)

    def tn(a, b):
        return lax.dot_general(a, b, TN, preferred_element_type=F32)

    def mm(a, b):
        return jnp.dot(a, b, preferred_element_type=F32)

    dkg[...] = jnp.zeros_like(dkg)
    dvg[...] = jnp.zeros_like(dvg)

    @pl.loop(0, 16)
    def _(i):
        rows = pl.ds(al(i * 128 + BLOCK, 64), 128)
        pick = (pos_t == i * 128 + lane).astype(F32).astype(BF)
        dkg[...] += mm(pick, r[1, rows])
        dvg[...] += mm(pick, r[2, rows])

    kg[...] = dkg[...].astype(BF)
    vg[...] = dvg[...].astype(BF)
    wz, wy = q_bufs[0], q_bufs[4]

    def saved(i):
        return (lax.div(i, 6), lax.rem(lax.div(i, 3), 2), pl.ds(al(lax.rem(i, 3) * 128, 128), 128))

    @pl.loop(0, 16)
    def _(i):
        rows = pl.ds(al(i * 128 + BLOCK, 64), 128)
        win = pl.ds(al(i * 128, 128), 256)
        q, k, v = r[0, rows], r[1, win], r[2, win]
        seen = masks[lax.div(i, 2), lax.rem(i, 2)]
        bias = jnp.where(low, seen[0:1], seen[1:2])
        sl = nt(q, k) * scale + bias
        sg = nt(q, kg[...]) * scale
        top = jnp.maximum(sl.max(-1, keepdims=True), sg.max(-1, keepdims=True))
        el, eg = jnp.exp(sl - top), jnp.exp(sg - top)
        inv = 1.0 / (el.sum(-1, keepdims=True) + eg.sum(-1, keepdims=True))
        plb, pgb = (el * inv).astype(BF), (eg * inv).astype(BF)
        a, b, rr = saved(i)
        wz[a, b, rr, pl.ds(0, 256)] = plb
        wz[a, b, rr, pl.ds(256, 128)] = pgb
        ctx = mm(plb, v) + mm(pgb, vg[...])
        j = lax.div(i, 2)
        wy[lax.div(j, 4), lax.rem(j, 4), pl.ds(al(lax.rem(i, 2) * 128, 128), 128), pl.ds(0, 128)] = ctx.astype(BF)

    def ctx_box(j):
        return wy.at[lax.div(j, 4), lax.rem(j, 4), pl.ds(0, 256), pl.ds(0, 128)]

    def spot(t0, n):
        rows = pl.ds(al(lax.div(me, 2) * CHIP_ROWS, CHIP_ROWS), CHIP_ROWS)
        return g.at[pl.ds(t0, n), rows, pl.ds(al(lax.rem(me, 2) * HDIM, HDIM), HDIM)]

    def spot_o():
        rows = pl.ds(al(lax.div(me, 2) * CHIP_ROWS, CHIP_ROWS), CHIP_ROWS)
        return g.at[3, rows, pl.ds(al(lax.rem(me, 2) * HDIM, HDIM), HDIM)]

    ctx_out = [
        remote(ctx_box(j), spot_o(), cssem.at[k], crsem.at[k], where) for k, (j, where) in enumerate(peers)
    ]
    for cp in ctx_out:
        cp.start()
    ctx_own = pltpu.make_async_copy(ctx_box(me), spot_o(), lsem.at[9])
    ctx_own.start()

    csend[5].wait_recv()
    back(xl)
    csend[6].wait_recv()
    back(xr)
    csend[3].wait_recv()
    csend[7].start()
    csend[4].wait_recv()
    csend[8].start()
    csend[7].wait_recv()
    csend[8].wait_recv()
    back(x2)

    at = {
        "up": up, "down": down, "yh": yh, "owner": c == p, "middle": c != p,
        "front": device(x, y, zr, c), "rear": device(x, y, zl, c),
        "above": device(x, up, z, c), "below": device(x, down, z, c),
    }
    groups = (z2, zr, zl, z)
    order = [(0, 0), (0, 1), (1, 1), (2, 0), (1, 0), (2, 1), (3, 0), (3, 1)]
    red_o = Reduce(at, HALF_O, o_bufs, o_sems)
    red_q = Reduce(at, HALF_Q, q_bufs, q_sems)

    def turn(t):
        for i in range(4):
            rows = pl.ds(i * 256, 256)
            gt[t, :, rows] = g[t, rows].T

    def piece(red, src, n, t0, count):
        o, ab = order[n]
        cols = pl.ds(al(ab * 2048 + groups[o] * 512, 512), 512)

        @pl.loop(0, count)
        def _(t):
            right_side = src[:, :, cols].reshape(1024, 512)
            acc = mm(gt[t0 + t], right_side).astype(BF)
            rows = pl.ds(al(t * 128, 128), 128)
            red.wz[o, ab, rows] = acc[:128]
            red.wy[ab, o, rows] = acc[128:]

        if n < 4:
            red.z[n].start()

    for j in range(8):

        @pl.when(j != me)
        def _():
            remote(box(j, 3), r.at[3, mine], bssem.at[j], brsem.at[j], sib).wait_send()

    pltpu.make_async_copy(box(me, 3), r.at[3, mine], lsem.at[7]).wait()
    for cp in ctx_out:
        cp.wait()
    ctx_own.wait()
    turn(3)
    for n in range(8):
        piece(red_o, cot, n, 3, 1)
    red_o.start_y()

    for j in range(8):

        @pl.when(j != me)
        def _():
            remote(box(j, 3), r.at[3, mine], bssem.at[j], brsem.at[j], sib).wait_recv()

    dkp[...] = jnp.zeros_like(dkp)
    dvp[...] = jnp.zeros_like(dvp)
    dkg[...] = jnp.zeros_like(dkg)
    dvg[...] = jnp.zeros_like(dvg)

    def out_box(i, t):
        j = lax.div(i, 2)
        return (t, pl.ds(al(lax.rem(i, 2) * 128, 128), 128), pl.ds(al(j * 128, 128), 128))

    @pl.loop(0, 16)
    def _(i):
        rows = pl.ds(al(i * 128 + BLOCK, 64), 128)
        win = pl.ds(al(i * 128, 128), 256)
        q, do, k, v = r[0, rows], r[3, rows], r[1, win], r[2, win]
        a, b, rr = saved(i)
        plb, pgb = wz[a, b, rr, pl.ds(0, 256)], wz[a, b, rr, pl.ds(256, 128)]
        dl, dg = nt(do, v), nt(do, vg[...])
        pf, pgf = plb.astype(F32), pgb.astype(F32)
        delta = (pf * dl).sum(-1, keepdims=True) + (pgf * dg).sum(-1, keepdims=True)
        sl = (pf * (dl - delta) * scale).astype(BF)
        sg = (pgf * (dg - delta) * scale).astype(BF)
        gt[out_box(i, 0)] = (mm(sl, k) + mm(sg, kg[...])).astype(BF)
        dkp[win] += tn(sl, q)
        dvp[win] += tn(plb, do)
        dkg[...] += tn(sg, q)
        dvg[...] += tn(pgb, do)

    def home(sems, t0, n):
        s, d = sems
        return [
            remote(boxes(j, t0, n), spot(t0, n), s.at[k], d.at[k], where) for k, (j, where) in enumerate(peers)
        ]

    home_q = home((dssem, drsem), 0, 1)
    for cp in home_q:
        cp.start()
    home_q_own = pltpu.make_async_copy(boxes(me, 0, 1), spot(0, 1), lsem.at[10])
    home_q_own.start()

    def split(a):
        high = a.astype(BF)
        return high, (a - high.astype(F32)).astype(BF)

    both = jnp.concatenate([jnp.concatenate(split(dkg[...]), 0), jnp.concatenate(split(dvg[...]), 0)], 1)

    @pl.loop(0, 16)
    def _(i):
        inner = pl.ds(al(i * 128 + BLOCK, 64), 128)
        put = (pos == i * 128 + sub).astype(F32).astype(BF)
        extra = mm(jnp.concatenate([put, put], 1), both)
        gt[out_box(i, 1)] = (dkp[inner] + extra[:, :128]).astype(BF)
        gt[out_box(i, 2)] = (dvp[inner] + extra[:, 128:]).astype(BF)

    home_kv = home((essem, ersem), 1, 2)
    for cp in home_kv:
        cp.start()
    home_kv_own = pltpu.make_async_copy(boxes(me, 1, 2), spot(1, 2), lsem.at[11])
    home_kv_own.start()

    red_o.dep_z()
    red_o.dep_y()
    for cp in tsend + csend + wsend:
        cp.wait_send()
    for cp in home_q + home_kv:
        cp.wait()
    home_q_own.wait()
    home_kv_own.wait()

    part = cot
    docs = (x2, xr, xl, x)
    to_sib = [remote(part.at[o, other], pr.at[o], sssem.at[o], srsem.at[o], sib) for o in range(4)]

    def tokens_part(o):
        rows = pl.ds(al(docs[o] * CHIP_ROWS, CHIP_ROWS), CHIP_ROWS)

        @pl.loop(0, 8)
        def _(n):
            cols = pl.ds(al(n * 512, 512), 512)
            a = jnp.concatenate([g[t, rows] for t in range(3)], 1)
            b = jnp.concatenate([w[t, cols] for t in range(3)], 1)
            part[o, :, cols] = nt(a, b).astype(BF)

        to_sib[o].start()

    xc = [
        remote(pr.at[0, pl.ds(0, 64)], xa.at[pl.ds(0, 64)], xssem.at[0], xrsem.at[0], right),
        remote(pr.at[0, pl.ds(64, 64)], xa.at[pl.ds(64, 64)], xssem.at[1], xrsem.at[1], left),
        remote(pr.at[1], xf.at[0], xssem.at[2], xrsem.at[2], right),
        remote(pr.at[2], xf.at[1], xssem.at[3], xrsem.at[3], left),
    ]

    def sum_rows(o, extra=None):
        @pl.loop(0, 8)
        def _(n):
            cols = pl.ds(al(n * 512, 512), 512)
            for h in range(2):
                rows = pl.ds(h * 64, 64)
                own_half = pl.ds(al(c * ROWS + h * 64, 64), 64)
                total = part[o, own_half, cols].astype(F32) + pr[o, rows, cols].astype(F32)
                if extra is not None and extra == h:
                    total += xa[rows, cols].astype(F32)
                pr[o, rows, cols] = total.astype(BF)

    tokens_part(0)
    for t in range(3):
        turn(t)
    for n in range(4):
        piece(red_q, tok, n, 0, 3)
    to_sib[0].wait_recv()
    sum_rows(0)
    xc[0].start()
    xc[1].start()
    for n in range(4, 8):
        piece(red_q, tok, n, 0, 3)
    red_q.start_y()
    for o in (1, 2, 3):
        tokens_part(o)
    red_q.dep_z()
    red_o.mid_z()
    red_o.mid_y()
    to_sib[1].wait_recv()
    xc[0].wait_recv()
    sum_rows(1, 0)
    xc[2].start()
    to_sib[2].wait_recv()
    xc[1].wait_recv()
    sum_rows(2, 1)
    xc[3].start()
    red_q.dep_y()
    red_o.last_z()
    red_o.last_y()
    to_sib[3].wait_recv()
    red_q.mid_z()
    red_q.mid_y()

    xc[2].wait_recv()
    xc[3].wait_recv()

    to_sib[3].wait_send()

    @pl.loop(0, 8)
    def _(n):
        cols = pl.ds(al(n * 512, 512), 512)
        total = part[3, own, cols].astype(F32) + pr[3, :, cols].astype(F32)
        total += xf[0, :, cols].astype(F32) + xf[1, :, cols].astype(F32)
        part[3, other, cols] = total.astype(BF)

    gt_copy = pltpu.make_async_copy(part.at[3, other], gt_out, lsem.at[12])
    gt_copy.start()
    red_q.last_z()
    red_q.last_y()

    outs = (gq_out, gk_out, gv_out, go_out)
    final = [remote(fs.at[1, t], outs[t], fssem.at[t], frsem.at[t], sib) for t in range(4)]
    final_own = [pltpu.make_async_copy(fs.at[0, t], outs[t], flsem.at[t]) for t in range(4)]

    @pl.when(c == p)
    def _():
        def put(t0):
            def run(head, n, value):
                lanes = pl.ds(head * 128, 128)
                for s in range(2):
                    core = c if s == 0 else 1 - c
                    got = value(pl.ds(al(core * 256, 256), 256))
                    if t0 + n < 3:
                        fs[s, n, :, lanes] = got.T
                    else:
                        fs[s, 3, lanes, :] = got

            return run

        red_o.result(put(3))
        final[3].start()
        final_own[3].start()
        red_q.result(put(0))
        for t in range(3):
            final[t].start()
            final_own[t].start()
        for t in range(4):
            final[t].wait_send()
            final_own[t].wait()

    @pl.when(c != p)
    def _():
        for cp in final:
            cp.wait_recv()

    red_o.drain()
    red_q.drain()
    for cp in to_sib[:3] + xc:
        cp.wait_send()
    gt_copy.wait()


def on_device(tokens, cotangent, w_query, w_key, w_value, w_output, global_pos, pattern):
    dma = pltpu.SemaphoreType.DMA
    vm = pltpu.VMEM
    square = jax.ShapeDtypeStruct((256, 256), F32)
    grad_tokens, gq, gk, gv, go = pl.pallas_call(
        kernel,
        out_shape=(jax.ShapeDtypeStruct((ROWS, D), BF), square, square, square, square),
        in_specs=[pl.BlockSpec(memory_space=pltpu.SMEM), pl.BlockSpec(memory_space=pltpu.VMEM)] + [ANY] * 6,
        out_specs=(ANY,) * 5,
        scratch_shapes=[
            vm((4, CHIP_ROWS, D), BF),
            vm((4, CHIP_ROWS, D), BF),
            vm((3, D, 256), BF),
            vm((256, D), BF),
            vm((4, 2176, HDIM), BF),
            vm((4, 1024, 256), BF),
            vm((4, 256, 1024), BF),
            vm((2, 8, 8, 256), F32),
            vm((8, 2, 8, 256), F32),
            vm((128, HDIM), BF), vm((128, HDIM), BF), vm((128, HDIM), F32), vm((128, HDIM), F32),
            vm((2176, HDIM), F32), vm((2176, HDIM), F32),
            vm((4, ROWS, D), BF),
            vm((ROWS, D), BF),
            vm((2, ROWS, D), BF),
            vm((2, 4, 256, 256), F32),
            *reduce_scratch(HALF_O),
            *reduce_scratch(HALF_Q),
            dma((2, 9)), dma((2, 9)), dma((4,)), dma((4, 2)), dma((13,)), dma((8,)), dma((8,)),
            dma((7,)), dma((7,)), dma((8,)), dma((8,)), dma((7,)), dma((7,)), dma((7,)), dma((7,)),
            dma((7,)), dma((7,)), dma((4,)), dma((4,)), dma((4,)), dma((4,)), dma((4,)), dma((4,)), dma((4,)),
        ],
        compiler_params=pltpu.CompilerParams(
            collective_id=0, has_side_effects=True, vmem_limit_bytes=63 << 20
        ),
        cost_estimate=pl.CostEstimate(flops=25 * 10**9, bytes_accessed=60 << 20, transcendentals=10**6),
    )(pattern, global_pos, tokens[0], cotangent[0], w_query, w_key, w_value, w_output)
    return grad_tokens[None], gq, gk, gv, go


def solution(mesh):
    in_specs = (
        P("fsdp", "seq", None),
        P("fsdp", "seq", None),
        P(None, "fsdp"),
        P(None, "fsdp"),
        P(None, "fsdp"),
        P("fsdp", None),
        P(),
        P(None, "seq", None),
    )
    out_specs = (
        P("fsdp", "seq", None),
        P("seq", "fsdp"),
        P("seq", "fsdp"),
        P("seq", "fsdp"),
        P("fsdp", "seq"),
    )
    return jax.shard_map(
        on_device, mesh=mesh, in_specs=in_specs, out_specs=out_specs, check_vma=False
    )
```

time: 282 us -> 207 us (0.73)
  Pallas kernels: 239 us -> 200 us
  blocking collectives: 27.2 us -> 0 us
  local copies, waits for them, and re-layouts: 14.1 us -> 6.56 us
    pallas_call x3 -> x1, Pallas kernels: 239 us -> 200 us  [on_device(): pl.pallas_call(kernel, out_shape=(jax.ShapeDtypeStruct((ROWS, D), BF), sq...]
    all_gather x1 -> x0, blocking collectives: 27.2 us -> none  [on_device(): flags = lax.all_gather(pattern, 'seq', axis=1, tiled=True)]
    unnamed x18 -> x14, local copies, waits for them, and re-layouts: 11.1 us -> 6.56 us
where the time goes in v2:
time: 207 us
  Pallas kernels  200 us (97%)
  local copies, waits for them, and re-layouts  6.56 us (3%)
    pallas_call x1, Pallas kernels, on_device(): pl.pallas_call(kernel, out_shape=(jax.ShapeDtypeStruct((ROWS, D), BF), sq...  200 us
    unnamed x14, local copies, waits for them, and re-layouts  6.56 us

profile of v2, /device:TPU:1, one launch (start us, length us, event | category | flops | bytes accessed | tf_op | source)
XLA Modules:
  0.0 206.9 jit_solution(11922159039183396771)
XLA Ops:
  0.6 1.4 copy.13.pat
  2.0 199.7 %shard_map.119 = (bf16[128,4096]{1,0:T(8,128)(2,1)}, f32[256,256]{1,0:T(8,128)}, f32[256,256]{1,0:T(8,128)}, f32[256,256]{1,0:T(8,128)}, f32[256,256]{1,0:T(8,128)}) custom-call(s32[8,2,2]{2,1,0:T(2,128)} %copy.13.pat, s32[8,128]{1,0:T(8,128)} %gpos.1, bf16[128,4096]{1,0:T(8,128)(2,1)} %bitcast.4, bf16[128,4096]{1,0:T(8,128)(2,1)} %bitcast.5, ...), custom_call_target="tpu_custom_call" | custom-call | flops 24999999488 | bytes 62914560 | tf_op jit(solution)/shard_map/pallas_call | solution.py:763
  201.7 0.0 copy-start.3
  201.7 0.0 copy-start.2
  201.7 0.0 copy-start.1
  201.7 0.0 copy-start
  201.7 2.4 %copy.19 = bf16[1,128,4096]{2,1,0:T(8,128)(2,1)} copy(bf16[1,128,4096]{2,1,0:T(8,128)(2,1)} %bitcast.3) | data formatting | bytes 2097152
  204.1 0.0 copy-done.3
  204.1 0.7 copy.20
  204.8 0.0 copy-done.2
  204.8 0.7 copy.21
  205.5 0.0 copy-done.1
  205.5 0.7 copy.22
  206.2 0.0 copy-done
  206.2 0.7 copy.23
Async XLA Ops:
  201.7 2.4 %copy-start.3 = (f32[256,256]{1,0:T(8,128)S(1)}, f32[256,256]{1,0:T(8,128)}, u32[]{:S(2)}) copy-start(f32[256,256]{1,0:T(8,128)} %get-tuple-element.21) | copy-start | bytes 786436
  201.7 3.1 %copy-start.2 = (f32[256,256]{1,0:T(8,128)S(1)}, f32[256,256]{1,0:T(8,128)}, u32[]{:S(2)}) copy-start(f32[256,256]{1,0:T(8,128)} %get-tuple-element.22) | copy-start | bytes 786436
  201.7 3.8 %copy-start.1 = (f32[256,256]{1,0:T(8,128)S(1)}, f32[256,256]{1,0:T(8,128)}, u32[]{:S(2)}) copy-start(f32[256,256]{1,0:T(8,128)} %get-tuple-element.23) | copy-start | bytes 786436
  201.7 4.5 %copy-start = (f32[256,256]{1,0:T(8,128)S(1)}, f32[256,256]{1,0:T(8,128)}, u32[]{:S(2)}) copy-start(f32[256,256]{1,0:T(8,128)} %get-tuple-element.24) | copy-start | bytes 786436

commit v3 on v2

--- a/solution.py
+++ b/solution.py
@@ -56,7 +56,7 @@
     return j, device(x, lax.div(j, 4) * 2 + lax.rem(y, 2), lax.rem(j, 4), c)
 
 
-HALF_Q, HALF_O = 384, 128
+HALF_KV, HALF_Q, HALF_O = 256, 128, 128
 
 
 class Reduce:
@@ -242,9 +242,9 @@
     tok, cot, w, wov, r, g, gt, mask, masks, kg, vg, dkg, dvg, dkp, dvp, pr, xa, xf, fs,
     *rest,
 ):
-    o_bufs, o_sems, q_bufs, q_sems = rest[:8], rest[8:10], rest[10:18], rest[18:20]
+    (o_bufs, o_sems), (q_bufs, q_sems), (v_bufs, v_sems) = [(rest[i : i + 8], rest[i + 8 : i + 10]) for i in (0, 10, 20)]
     (ssem, rsem, wssem, wrsem, lsem, mssem, mrsem, assem, arsem, bssem, brsem,
-     cssem, crsem, dssem, drsem, essem, ersem, sssem, srsem, xssem, xrsem, fssem, frsem, flsem) = rest[20:]
+     cssem, crsem, dssem, drsem, essem, ersem, sssem, srsem, xssem, xrsem, fssem, frsem, flsem) = rest[30:]
     x, y, z, c = place()
     p, yh = lax.rem(y, 2), lax.div(y, 2)
     seq = lax.axis_index("seq")
@@ -257,22 +257,6 @@
     my_doc = lax.div(me, 2) * 2 + p
     peers = [chip_peer(x, y, z, c, k) for k in range(1, 8)]
 
-    kb = lax.div(lax.broadcasted_iota(jnp.int32, (8, 256), 1), 64)
-    upper = lax.broadcasted_iota(jnp.int32, (8, 256), 0) == 0
-
-    @pl.loop(0, 8)
-    def _(d):
-        prev0 = jnp.where(seq > 0, pat[d, 0, 0], 0)
-        next0, prev1 = pat[d, 0, 1], pat[d, 1, 0]
-        next1 = jnp.where(seq < 15, pat[d, 1, 1], 0)
-        m0 = jnp.where(kb == 0, prev0, jnp.where(kb == 1, 1, jnp.where(kb == 2, next0, 0)))
-        m1 = jnp.where(kb == 0, 0, jnp.where(kb == 1, prev1, jnp.where(kb == 2, 1, next1)))
-        mask[c, d] = jnp.where(jnp.where(upper, m0, m1) == 1, 0.0, -jnp.inf)
-
-    for t in (1, 2):
-        r[t, :BLOCK] = jnp.zeros((BLOCK, HDIM), BF)
-        r[t, BLOCK + 2048 :] = jnp.zeros((BLOCK, HDIM), BF)
-
     meet(
         [right, left, sib]
         + [device(x, v, z, core) for v in (up, down) for core in (0, 1)]
@@ -302,13 +286,33 @@
     tsend = sends(0, tok_in, tok)
     csend = sends(1, cot_in, cot)
     wdev = device(x, mod4(y + 1 + 2 * c), z, p)
-    half = pl.ds(al(c * 2048, 2048), 2048)
-    half_o = pl.ds(al(c * 128, 128), 128)
+    zhalf = lax.rem(z, 2)
+    sources = (wq, wk, wv, wo)
+
+    def quarter(t, ref, h, n):
+        size = 1024 if t < 3 else 64
+        rows = pl.ds(al((2 * h + n) * size, size), size)
+        return ref.at[t, rows] if ref is w else ref.at[rows]
+
+    def held(t):
+        return w if t < 3 else wov
+
     wsend = [
-        remote(src.at[half], w.at[t, half], wssem.at[t], wrsem.at[t, c], wdev)
-        for t, src in enumerate((wq, wk, wv))
+        remote(quarter(t, src, zhalf, c), quarter(t, held(t), zhalf, c), wssem.at[t], wrsem.at[t, c], wdev)
+        for t, src in enumerate(sources)
     ]
-    wsend.append(remote(wo.at[half_o], wov.at[half_o], wssem.at[3], wrsem.at[3, c], wdev))
+    zdev = (device(x, y, zr, c), device(x, y, zl, c))
+    wpass = [
+        [
+            remote(
+                quarter(t, held(t), zhalf, n), quarter(t, held(t), zhalf, n),
+                wssem.at[4 + 2 * t + n], wrsem.at[4 + t, n], zdev[n],
+            )
+            for n in (0, 1)
+        ]
+        for t in range(4)
+    ]
+
     wlocal = [pltpu.make_async_copy(src, w.at[t], lsem.at[t]) for t, src in enumerate((wq, wk, wv))]
     wlocal.append(pltpu.make_async_copy(wo, wov, lsem.at[3]))
     tlocal = pltpu.make_async_copy(tok_in, tok.at[x, own], lsem.at[4])
@@ -325,6 +329,22 @@
     def _():
         for cp in wlocal:
             cp.start()
+
+    kb = lax.div(lax.broadcasted_iota(jnp.int32, (8, 256), 1), 64)
+    upper = lax.broadcasted_iota(jnp.int32, (8, 256), 0) == 0
+
+    @pl.loop(0, 8)
+    def _(d):
+        prev0 = jnp.where(seq > 0, pat[d, 0, 0], 0)
+        next0, prev1 = pat[d, 0, 1], pat[d, 1, 0]
+        next1 = jnp.where(seq < 15, pat[d, 1, 1], 0)
+        m0 = jnp.where(kb == 0, prev0, jnp.where(kb == 1, 1, jnp.where(kb == 2, next0, 0)))
+        m1 = jnp.where(kb == 0, 0, jnp.where(kb == 1, prev1, jnp.where(kb == 2, 1, next1)))
+        mask[c, d] = jnp.where(jnp.where(upper, m0, m1) == 1, 0.0, -jnp.inf)
+
+    for t in (1, 2):
+        r[t, :BLOCK] = jnp.zeros((BLOCK, HDIM), BF)
+        r[t, BLOCK + 2048 :] = jnp.zeros((BLOCK, HDIM), BF)
 
     mask_sib = remote(mask.at[c], mask.at[c], mssem.at[7], mrsem.at[7], sib)
     mask_sib.start()
@@ -346,59 +366,88 @@
         copies[4].start()
         copies[6].start()
 
+    def weights_pass():
+        @pl.when(c != p)
+        def _():
+            for t in range(4):
+                for n in (0, 1):
+                    ref = quarter(t, held(t), zhalf, n)
+                    remote(ref, ref, wssem.at[t], wrsem.at[t, n], sib).wait_recv()
+                    wpass[t][n].start()
+
+    def weights_here(ts):
+        @pl.when(c == p)
+        def _():
+            for t in ts:
+                wlocal[t].wait()
+
+        @pl.when(c != p)
+        def _():
+            for t in ts:
+                for n in (0, 1):
+                    wpass[t][n].wait()
+
+    mine = pl.ds(al(me * CHIP_ROWS + BLOCK, 64), CHIP_ROWS)
+
+    def boxes(j, t0, n):
+        return gt.at[pl.ds(t0, n), :, pl.ds(al(j * HDIM, HDIM), HDIM)]
+
+    def box(j, t):
+        return gt.at[t, :, pl.ds(al(j * HDIM, HDIM), HDIM)]
+
+    def chip(j):
+        return device(x, lax.div(j, 4) * 2 + p, lax.rem(j, 4), c)
+
+    def project(doc, ts):
+        for t in ts:
+            got = jnp.dot(tok[doc], w[t], preferred_element_type=F32).astype(BF)
+            gt[t, :, pl.ds(al(doc * 256, 256), 256)] = got
+
+    def qkv(j):
+        return remote(boxes(j, 0, 3), r.at[pl.ds(0, 3), mine], assem.at[j], arsem.at[me], chip(j))
+
+    qkv_own = pltpu.make_async_copy(boxes(me, 0, 3), r.at[pl.ds(0, 3), mine], lsem.at[6])
+
+    def send_qkv(doc):
+        for h in (0, 1):
+            j = 2 * doc + h
+
+            @pl.when(j != me)
+            def _():
+                qkv(j).start()
+
+            @pl.when(j == me)
+            def _():
+                qkv_own.start()
+
+    weights_pass()
     relay(tsend)
     for k in (0, 1, 2):
         csend[k].start()
+    tlocal.wait()
+    clocal.wait()
+    tsend[2].wait_recv()
+    tsend[5].wait_recv()
+    tsend[6].wait_recv()
+    near = (x, xl, xr)
+    weights_here((0,))
+    for doc in near:
+        project(doc, (0,))
+    weights_here((1,))
+    for doc in near:
+        project(doc, (1,))
     tsend[3].wait_recv()
     tsend[7].start()
     tsend[4].wait_recv()
     tsend[8].start()
-    tlocal.wait()
-    clocal.wait()
-
-    def weights_here(ts):
-        @pl.when(c == p)
-        def _():
-            for t in ts:
-                wlocal[t].wait()
-
-        @pl.when(c != p)
-        def _():
-            for t in ts:
-                for h in (0, 1):
-                    if t < 3:
-                        ref = w.at[t, pl.ds(h * 2048, 2048)]
-                    else:
-                        ref = wov.at[pl.ds(h * 128, 128)]
-                    remote(ref, ref, wssem.at[t], wrsem.at[t, h], sib).wait_recv()
-
-    weights_here((0, 1, 2))
-    for k in (2, 5, 6, 7, 8):
-        tsend[k].wait_recv()
-
-    def box(j, t):
-        return gt.at[t, :, pl.ds(al(j * HDIM, HDIM), HDIM)]
-
-    @pl.loop(0, 4)
-    def _(doc):
-        @pl.loop(0, 3)
-        def _(t):
-            got = jnp.dot(tok[doc], w[t], preferred_element_type=F32).astype(BF)
-            gt[t, :, pl.ds(al(doc * 256, 256), 256)] = got
-
-    mine = pl.ds(al(me * CHIP_ROWS + BLOCK, 64), CHIP_ROWS)
-
-    def boxes(j, t0, n):
-        return gt.at[pl.ds(t0, n), :, pl.ds(al(j * HDIM, HDIM), HDIM)]
-
-    qkv = [
-        remote(boxes(j, 0, 3), r.at[pl.ds(0, 3), mine], assem.at[k], arsem.at[k], where)
-        for k, (j, where) in enumerate(peers)
-    ]
-    for cp in qkv:
-        cp.start()
-    qkv_own = pltpu.make_async_copy(boxes(me, 0, 3), r.at[pl.ds(0, 3), mine], lsem.at[6])
-    qkv_own.start()
+    weights_here((2,))
+    for doc in near:
+        project(doc, (2,))
+        send_qkv(doc)
+    tsend[7].wait_recv()
+    tsend[8].wait_recv()
+    project(x2, (0, 1, 2))
+    send_qkv(x2)
 
     relay(csend)
     weights_here((3,))
@@ -408,11 +457,10 @@
         gt[3, :, pl.ds(al(doc * 256, 256), 256)] = got
         for h in (0, 1):
             j = 2 * doc + h
-            where = device(x, lax.div(j, 4) * 2 + p, lax.rem(j, 4), c)
 
             @pl.when(j != me)
             def _():
-                remote(box(j, 3), r.at[3, mine], bssem.at[j], brsem.at[me], where).start()
+                remote(box(j, 3), r.at[3, mine], bssem.at[j], brsem.at[me], chip(j)).start()
 
             @pl.when(j == me)
             def _():
@@ -420,9 +468,15 @@
 
     csend[2].wait_recv()
     back(x)
-
-    for cp in qkv:
-        cp.wait()
+    csend[5].wait_recv()
+    back(xl)
+    csend[6].wait_recv()
+    back(xr)
+
+    for n in range(1, 8):
+        j = lax.rem(me + n, 8)
+        qkv(j).wait_send()
+        remote(boxes(j, 0, 3), r.at[pl.ds(0, 3), mine], assem.at[j], arsem.at[j], sib).wait_recv()
     qkv_own.wait()
     for cp in mask_out:
         cp.wait()
@@ -455,10 +509,10 @@
 
     kg[...] = dkg[...].astype(BF)
     vg[...] = dvg[...].astype(BF)
-    wz, wy = q_bufs[0], q_bufs[4]
+    wz, wy = v_bufs[0], v_bufs[4]
 
     def saved(i):
-        return (lax.div(i, 6), lax.rem(lax.div(i, 3), 2), pl.ds(al(lax.rem(i, 3) * 128, 128), 128))
+        return (lax.div(i, 4), lax.rem(lax.div(i, 2), 2), pl.ds(al(lax.rem(i, 2) * 128, 128), 128))
 
     @pl.loop(0, 16)
     def _(i):
@@ -499,10 +553,6 @@
     ctx_own = pltpu.make_async_copy(ctx_box(me), spot_o(), lsem.at[9])
     ctx_own.start()
 
-    csend[5].wait_recv()
-    back(xl)
-    csend[6].wait_recv()
-    back(xr)
     csend[3].wait_recv()
     csend[7].start()
     csend[4].wait_recv()
@@ -520,6 +570,7 @@
     order = [(0, 0), (0, 1), (1, 1), (2, 0), (1, 0), (2, 1), (3, 0), (3, 1)]
     red_o = Reduce(at, HALF_O, o_bufs, o_sems)
     red_q = Reduce(at, HALF_Q, q_bufs, q_sems)
+    red_v = Reduce(at, HALF_KV, v_bufs, v_sems)
 
     def turn(t):
         for i in range(4):
@@ -548,13 +599,6 @@
             remote(box(j, 3), r.at[3, mine], bssem.at[j], brsem.at[j], sib).wait_send()
 
     pltpu.make_async_copy(box(me, 3), r.at[3, mine], lsem.at[7]).wait()
-    for cp in ctx_out:
-        cp.wait()
-    ctx_own.wait()
-    turn(3)
-    for n in range(8):
-        piece(red_o, cot, n, 3, 1)
-    red_o.start_y()
 
     for j in range(8):
 
@@ -571,8 +615,7 @@
         j = lax.div(i, 2)
         return (t, pl.ds(al(lax.rem(i, 2) * 128, 128), 128), pl.ds(al(j * 128, 128), 128))
 
-    @pl.loop(0, 16)
-    def _(i):
+    def backward(i):
         rows = pl.ds(al(i * 128 + BLOCK, 64), 128)
         win = pl.ds(al(i * 128, 128), 256)
         q, do, k, v = r[0, rows], r[3, rows], r[1, win], r[2, win]
@@ -589,17 +632,28 @@
         dkg[...] += tn(sg, q)
         dvg[...] += tn(pgb, do)
 
+    def home_q(j):
+        return remote(box(j, 0), spot(0, 1).at[0], dssem.at[j], drsem.at[me], chip(j))
+
+    home_q_own = pltpu.make_async_copy(box(me, 0), spot(0, 1).at[0], lsem.at[10])
+
+    @pl.loop(1, 9)
+    def _(n):
+        j = lax.rem(me + n, 8)
+        backward(2 * j)
+        backward(2 * j + 1)
+
+        @pl.when(n < 8)
+        def _():
+            home_q(j).start()
+
+    home_q_own.start()
+
     def home(sems, t0, n):
         s, d = sems
         return [
             remote(boxes(j, t0, n), spot(t0, n), s.at[k], d.at[k], where) for k, (j, where) in enumerate(peers)
         ]
-
-    home_q = home((dssem, drsem), 0, 1)
-    for cp in home_q:
-        cp.start()
-    home_q_own = pltpu.make_async_copy(boxes(me, 0, 1), spot(0, 1), lsem.at[10])
-    home_q_own.start()
 
     def split(a):
         high = a.astype(BF)
@@ -621,13 +675,22 @@
     home_kv_own = pltpu.make_async_copy(boxes(me, 1, 2), spot(1, 2), lsem.at[11])
     home_kv_own.start()
 
-    red_o.dep_z()
-    red_o.dep_y()
+    for cp in ctx_out:
+        cp.wait()
+    ctx_own.wait()
+    turn(3)
+    for n in range(8):
+        piece(red_o, cot, n, 3, 1)
+    red_o.start_y()
     for cp in tsend + csend + wsend:
         cp.wait_send()
-    for cp in home_q + home_kv:
+    for n in range(1, 8):
+        j = lax.rem(me + n, 8)
+        home_q(j).wait_send()
+        remote(box(j, 0), spot(0, 1).at[0], dssem.at[j], drsem.at[j], sib).wait_recv()
+    home_q_own.wait()
+    for cp in home_kv:
         cp.wait()
-    home_q_own.wait()
     home_kv_own.wait()
 
     part = cot
@@ -666,22 +729,25 @@
                 pr[o, rows, cols] = total.astype(BF)
 
     tokens_part(0)
-    for t in range(3):
-        turn(t)
-    for n in range(4):
-        piece(red_q, tok, n, 0, 3)
+    tokens_part(1)
     to_sib[0].wait_recv()
     sum_rows(0)
     xc[0].start()
     xc[1].start()
+    turn(0)
+    for n in range(8):
+        piece(red_q, tok, n, 0, 1)
+    red_q.start_y()
+    tokens_part(2)
+    turn(1)
+    turn(2)
+    for n in range(4):
+        piece(red_v, tok, n, 1, 2)
+    red_o.dep_z()
+    red_o.dep_y()
     for n in range(4, 8):
-        piece(red_q, tok, n, 0, 3)
-    red_q.start_y()
-    for o in (1, 2, 3):
-        tokens_part(o)
-    red_q.dep_z()
-    red_o.mid_z()
-    red_o.mid_y()
+        piece(red_v, tok, n, 1, 2)
+    red_v.start_y()
     to_sib[1].wait_recv()
     xc[0].wait_recv()
     sum_rows(1, 0)
@@ -690,12 +756,22 @@
     xc[1].wait_recv()
     sum_rows(2, 1)
     xc[3].start()
+    red_q.dep_z()
     red_q.dep_y()
+    red_o.mid_z()
+    red_o.mid_y()
+    tokens_part(3)
+    red_v.dep_z()
+    red_v.dep_y()
     red_o.last_z()
     red_o.last_y()
-    to_sib[3].wait_recv()
     red_q.mid_z()
     red_q.mid_y()
+    red_q.last_z()
+    red_q.last_y()
+    to_sib[3].wait_recv()
+    red_v.mid_z()
+    red_v.mid_y()
 
     xc[2].wait_recv()
     xc[3].wait_recv()
@@ -711,8 +787,8 @@
 
     gt_copy = pltpu.make_async_copy(part.at[3, other], gt_out, lsem.at[12])
     gt_copy.start()
-    red_q.last_z()
-    red_q.last_y()
+    red_v.last_z()
+    red_v.last_y()
 
     outs = (gq_out, gk_out, gv_out, go_out)
     final = [remote(fs.at[1, t], outs[t], fssem.at[t], frsem.at[t], sib) for t in range(4)]
@@ -727,7 +803,7 @@
                     core = c if s == 0 else 1 - c
                     got = value(pl.ds(al(core * 256, 256), 256))
                     if t0 + n < 3:
-                        fs[s, n, :, lanes] = got.T
+                        fs[s, t0 + n, :, lanes] = got.T
                     else:
                         fs[s, 3, lanes, :] = got
 
@@ -737,7 +813,10 @@
         final[3].start()
         final_own[3].start()
         red_q.result(put(0))
-        for t in range(3):
+        final[0].start()
+        final_own[0].start()
+        red_v.result(put(1))
+        for t in (1, 2):
             final[t].start()
             final_own[t].start()
         for t in range(4):
@@ -751,6 +830,7 @@
 
     red_o.drain()
     red_q.drain()
+    red_v.drain()
     for cp in to_sib[:3] + xc:
         cp.wait_send()
     gt_copy.wait()
@@ -783,8 +863,9 @@
             vm((2, 4, 256, 256), F32),
             *reduce_scratch(HALF_O),
             *reduce_scratch(HALF_Q),
-            dma((2, 9)), dma((2, 9)), dma((4,)), dma((4, 2)), dma((13,)), dma((8,)), dma((8,)),
-            dma((7,)), dma((7,)), dma((8,)), dma((8,)), dma((7,)), dma((7,)), dma((7,)), dma((7,)),
+            *reduce_scratch(HALF_KV),
+            dma((2, 9)), dma((2, 9)), dma((12,)), dma((8, 2)), dma((13,)), dma((8,)), dma((8,)),
+            dma((8,)), dma((8,)), dma((8,)), dma((8,)), dma((7,)), dma((7,)), dma((8,)), dma((8,)),
             dma((7,)), dma((7,)), dma((4,)), dma((4,)), dma((4,)), dma((4,)), dma((4,)), dma((4,)), dma((4,)),
         ],
         compiler_params=pltpu.CompilerParams(

time: 207 us -> 193 us (0.932)
  Pallas kernels: 200 us -> 185 us
    pallas_call x1, Pallas kernels: 200 us -> 185 us  [on_device(): pl.pallas_call(kernel, out_shape=(jax.ShapeDtypeStruct((ROWS, D), BF), sq...]
where the time goes in v3:
time: 193 us
  Pallas kernels  185 us (96%)
  local copies, waits for them, and re-layouts  6.56 us (3%)
    pallas_call x1, Pallas kernels, on_device(): pl.pallas_call(kernel, out_shape=(jax.ShapeDtypeStruct((ROWS, D), BF), sq...  185 us
    unnamed x14, local copies, waits for them, and re-layouts  6.56 us

profile of v3, /device:TPU:1, one launch (start us, length us, event | category | flops | bytes accessed | tf_op | source)
XLA Modules:
  0.0 192.5 jit_solution(17214286106596827403)
XLA Ops:
  0.6 1.4 copy.13.pat
  2.0 185.3 %shard_map.119 = (bf16[128,4096]{1,0:T(8,128)(2,1)}, f32[256,256]{1,0:T(8,128)}, f32[256,256]{1,0:T(8,128)}, f32[256,256]{1,0:T(8,128)}, f32[256,256]{1,0:T(8,128)}) custom-call(s32[8,2,2]{2,1,0:T(2,128)} %copy.13.pat, s32[8,128]{1,0:T(8,128)} %gpos.1, bf16[128,4096]{1,0:T(8,128)(2,1)} %bitcast.4, bf16[128,4096]{1,0:T(8,128)(2,1)} %bitcast.5, ...), custom_call_target="tpu_custom_call" | custom-call | flops 24999999488 | bytes 62914560 | tf_op jit(solution)/shard_map/pallas_call | solution.py:843
  187.3 0.0 copy-start.3
  187.3 0.0 copy-start.2
  187.3 0.0 copy-start.1
  187.3 0.0 copy-start
  187.3 2.4 %copy.19 = bf16[1,128,4096]{2,1,0:T(8,128)(2,1)} copy(bf16[1,128,4096]{2,1,0:T(8,128)(2,1)} %bitcast.3) | data formatting | bytes 2097152
  189.7 0.0 copy-done.3
  189.7 0.7 copy.20
  190.4 0.0 copy-done.2
  190.4 0.7 copy.21
  191.1 0.0 copy-done.1
  191.1 0.7 copy.22
  191.8 0.0 copy-done
  191.8 0.7 copy.23
Async XLA Ops:
  187.3 2.4 %copy-start.3 = (f32[256,256]{1,0:T(8,128)S(1)}, f32[256,256]{1,0:T(8,128)}, u32[]{:S(2)}) copy-start(f32[256,256]{1,0:T(8,128)} %get-tuple-element.21) | copy-start | bytes 786436
  187.3 3.1 %copy-start.2 = (f32[256,256]{1,0:T(8,128)S(1)}, f32[256,256]{1,0:T(8,128)}, u32[]{:S(2)}) copy-start(f32[256,256]{1,0:T(8,128)} %get-tuple-element.22) | copy-start | bytes 786436
  187.3 3.8 %copy-start.1 = (f32[256,256]{1,0:T(8,128)S(1)}, f32[256,256]{1,0:T(8,128)}, u32[]{:S(2)}) copy-start(f32[256,256]{1,0:T(8,128)} %get-tuple-element.23) | copy-start | bytes 786436
  187.3 4.5 %copy-start = (f32[256,256]{1,0:T(8,128)S(1)}, f32[256,256]{1,0:T(8,128)}, u32[]{:S(2)}) copy-start(f32[256,256]{1,0:T(8,128)} %get-tuple-element.24) | copy-start | bytes 786436

commit v4 on v3

--- a/solution.py
+++ b/solution.py
@@ -398,27 +398,36 @@
     def chip(j):
         return device(x, lax.div(j, 4) * 2 + p, lax.rem(j, 4), c)
 
-    def project(doc, ts):
-        for t in ts:
-            got = jnp.dot(tok[doc], w[t], preferred_element_type=F32).astype(BF)
-            gt[t, :, pl.ds(al(doc * 256, 256), 256)] = got
+    def project(doc, t):
+        got = jnp.dot(tok[doc], w[t], preferred_element_type=F32).astype(BF)
+        gt[t, :, pl.ds(al(doc * 256, 256), 256)] = got
+
+    def project_near(t):
+        @pl.loop(0, 3)
+        def _(n):
+            project(lax.rem(x + n + lax.div(n, 2), 4), t)
 
     def qkv(j):
         return remote(boxes(j, 0, 3), r.at[pl.ds(0, 3), mine], assem.at[j], arsem.at[me], chip(j))
 
     qkv_own = pltpu.make_async_copy(boxes(me, 0, 3), r.at[pl.ds(0, 3), mine], lsem.at[6])
 
-    def send_qkv(doc):
-        for h in (0, 1):
-            j = 2 * doc + h
-
-            @pl.when(j != me)
-            def _():
-                qkv(j).start()
-
-            @pl.when(j == me)
-            def _():
-                qkv_own.start()
+    def send_qkv(last):
+        for n in range(8):
+            j = lax.rem(me + n, 8)
+            here = lax.div(j, 2) == x2
+            here = here if last else jnp.logical_not(here)
+            if n == 0:
+
+                @pl.when(here)
+                def _():
+                    qkv_own.start()
+
+            else:
+
+                @pl.when(here)
+                def _():
+                    qkv(j).start()
 
     weights_pass()
     relay(tsend)
@@ -429,25 +438,25 @@
     tsend[2].wait_recv()
     tsend[5].wait_recv()
     tsend[6].wait_recv()
-    near = (x, xl, xr)
     weights_here((0,))
-    for doc in near:
-        project(doc, (0,))
+    project_near(0)
     weights_here((1,))
-    for doc in near:
-        project(doc, (1,))
+    project_near(1)
     tsend[3].wait_recv()
     tsend[7].start()
     tsend[4].wait_recv()
     tsend[8].start()
     weights_here((2,))
-    for doc in near:
-        project(doc, (2,))
-        send_qkv(doc)
+    project_near(2)
+    send_qkv(False)
     tsend[7].wait_recv()
     tsend[8].wait_recv()
-    project(x2, (0, 1, 2))
-    send_qkv(x2)
+
+    @pl.loop(0, 3)
+    def _(t):
+        project(x2, t)
+
+    send_qkv(True)
 
     relay(csend)
     weights_here((3,))
@@ -514,25 +523,40 @@
     def saved(i):
         return (lax.div(i, 4), lax.rem(lax.div(i, 2), 2), pl.ds(al(lax.rem(i, 2) * 128, 128), 128))
 
-    @pl.loop(0, 16)
-    def _(i):
-        rows = pl.ds(al(i * 128 + BLOCK, 64), 128)
-        win = pl.ds(al(i * 128, 128), 256)
-        q, k, v = r[0, rows], r[1, win], r[2, win]
-        seen = masks[lax.div(i, 2), lax.rem(i, 2)]
-        bias = jnp.where(low, seen[0:1], seen[1:2])
-        sl = nt(q, k) * scale + bias
-        sg = nt(q, kg[...]) * scale
-        top = jnp.maximum(sl.max(-1, keepdims=True), sg.max(-1, keepdims=True))
-        el, eg = jnp.exp(sl - top), jnp.exp(sg - top)
-        inv = 1.0 / (el.sum(-1, keepdims=True) + eg.sum(-1, keepdims=True))
-        plb, pgb = (el * inv).astype(BF), (eg * inv).astype(BF)
-        a, b, rr = saved(i)
-        wz[a, b, rr, pl.ds(0, 256)] = plb
-        wz[a, b, rr, pl.ds(256, 128)] = pgb
-        ctx = mm(plb, v) + mm(pgb, vg[...])
-        j = lax.div(i, 2)
-        wy[lax.div(j, 4), lax.rem(j, 4), pl.ds(al(lax.rem(i, 2) * 128, 128), 128), pl.ds(0, 128)] = ctx.astype(BF)
+    def forward(j):
+        tiles = (2 * j, 2 * j + 1)
+        rows = [pl.ds(al(i * 128 + BLOCK, 64), 128) for i in tiles]
+        wins = [pl.ds(al(i * 128, 128), 256) for i in tiles]
+        qs = [r[0, a] for a in rows]
+        ks, vs = [r[1, a] for a in wins], [r[2, a] for a in wins]
+        kgv, vgv = kg[...], vg[...]
+        sls = [nt(q, k) for q, k in zip(qs, ks)]
+        sgs = [nt(q, kgv) * scale for q in qs]
+        for h in (0, 1):
+            seen = masks[j, h]
+            sls[h] = sls[h] * scale + jnp.where(low, seen[0:1], seen[1:2])
+        tops = [jnp.maximum(a.max(-1, keepdims=True), b.max(-1, keepdims=True)) for a, b in zip(sls, sgs)]
+        els = [jnp.exp(a - t) for a, t in zip(sls, tops)]
+        egs = [jnp.exp(a - t) for a, t in zip(sgs, tops)]
+        invs = [1.0 / (a.sum(-1, keepdims=True) + b.sum(-1, keepdims=True)) for a, b in zip(els, egs)]
+        pls = [(a * t).astype(BF) for a, t in zip(els, invs)]
+        pgs = [(a * t).astype(BF) for a, t in zip(egs, invs)]
+        ctx = [(mm(a, v) + mm(b, vgv)).astype(BF) for a, b, v in zip(pls, pgs, vs)]
+        for h in (0, 1):
+            a, b, rr = saved(tiles[h])
+            wz[a, b, rr, pl.ds(0, 256)] = pls[h]
+            wz[a, b, rr, pl.ds(256, 128)] = pgs[h]
+            wy[lax.div(j, 4), lax.rem(j, 4), pl.ds(h * 128, 128), pl.ds(0, 128)] = ctx[h]
+
+    pl.loop(0, 5)(forward)
+    csend[3].wait_recv()
+    csend[7].start()
+    csend[4].wait_recv()
+    csend[8].start()
+    csend[7].wait_recv()
+    csend[8].wait_recv()
+    back(x2)
+    pl.loop(5, 8)(forward)
 
     def ctx_box(j):
         return wy.at[lax.div(j, 4), lax.rem(j, 4), pl.ds(0, 256), pl.ds(0, 128)]
@@ -552,14 +576,6 @@
         cp.start()
     ctx_own = pltpu.make_async_copy(ctx_box(me), spot_o(), lsem.at[9])
     ctx_own.start()
-
-    csend[3].wait_recv()
-    csend[7].start()
-    csend[4].wait_recv()
-    csend[8].start()
-    csend[7].wait_recv()
-    csend[8].wait_recv()
-    back(x2)
 
     at = {
         "up": up, "down": down, "yh": yh, "owner": c == p, "middle": c != p,
@@ -579,15 +595,17 @@
 
     def piece(red, src, n, t0, count):
         o, ab = order[n]
-        cols = pl.ds(al(ab * 2048 + groups[o] * 512, 512), 512)
-
-        @pl.loop(0, count)
-        def _(t):
-            right_side = src[:, :, cols].reshape(1024, 512)
-            acc = mm(gt[t0 + t], right_side).astype(BF)
-            rows = pl.ds(al(t * 128, 128), 128)
-            red.wz[o, ab, rows] = acc[:128]
-            red.wy[ab, o, rows] = acc[128:]
+
+        @pl.loop(0, 2)
+        def _(h):
+            lanes = pl.ds(al(h * 256, 256), 256)
+            here = pl.ds(al(ab * 2048 + groups[o] * 512 + h * 256, 256), 256)
+            left_side = gt[pl.ds(t0, count)].reshape(count * 256, 1024)
+            acc = mm(left_side, src[:, :, here].reshape(1024, 256)).astype(BF)
+            for t in range(count):
+                rows = pl.ds(t * 128, 128)
+                red.wz[o, ab, rows, lanes] = acc[t * 256 : t * 256 + 128]
+                red.wy[ab, o, rows, lanes] = acc[t * 256 + 128 : t * 256 + 256]
 
         if n < 4:
             red.z[n].start()
@@ -615,22 +633,36 @@
         j = lax.div(i, 2)
         return (t, pl.ds(al(lax.rem(i, 2) * 128, 128), 128), pl.ds(al(j * 128, 128), 128))
 
-    def backward(i):
-        rows = pl.ds(al(i * 128 + BLOCK, 64), 128)
-        win = pl.ds(al(i * 128, 128), 256)
-        q, do, k, v = r[0, rows], r[3, rows], r[1, win], r[2, win]
-        a, b, rr = saved(i)
-        plb, pgb = wz[a, b, rr, pl.ds(0, 256)], wz[a, b, rr, pl.ds(256, 128)]
-        dl, dg = nt(do, v), nt(do, vg[...])
-        pf, pgf = plb.astype(F32), pgb.astype(F32)
-        delta = (pf * dl).sum(-1, keepdims=True) + (pgf * dg).sum(-1, keepdims=True)
-        sl = (pf * (dl - delta) * scale).astype(BF)
-        sg = (pgf * (dg - delta) * scale).astype(BF)
-        gt[out_box(i, 0)] = (mm(sl, k) + mm(sg, kg[...])).astype(BF)
-        dkp[win] += tn(sl, q)
-        dvp[win] += tn(plb, do)
-        dkg[...] += tn(sg, q)
-        dvg[...] += tn(pgb, do)
+    def backward(j):
+        tiles = (2 * j, 2 * j + 1)
+        rows = [pl.ds(al(i * 128 + BLOCK, 64), 128) for i in tiles]
+        wins = [pl.ds(al(i * 128, 128), 256) for i in tiles]
+        qs, dos = [r[0, a] for a in rows], [r[3, a] for a in rows]
+        ks, vs = [r[1, a] for a in wins], [r[2, a] for a in wins]
+        kgv, vgv = kg[...], vg[...]
+        spots = [saved(i) for i in tiles]
+        pls = [wz[a, b, rr, pl.ds(0, 256)] for a, b, rr in spots]
+        pgs = [wz[a, b, rr, pl.ds(256, 128)] for a, b, rr in spots]
+        dls = [nt(d, v) for d, v in zip(dos, vs)]
+        dgs = [nt(d, vgv) for d in dos]
+        dvl = [tn(a, d) for a, d in zip(pls, dos)]
+        dvs = tn(jnp.concatenate(pgs, 0), jnp.concatenate(dos, 0))
+        pfs, pgf = [a.astype(F32) for a in pls], [a.astype(F32) for a in pgs]
+        deltas = [
+            (a * d).sum(-1, keepdims=True) + (b * e).sum(-1, keepdims=True) for a, d, b, e in zip(pfs, dls, pgf, dgs)
+        ]
+        sls = [(a * (d - t) * scale).astype(BF) for a, d, t in zip(pfs, dls, deltas)]
+        sgs = [(a * (d - t) * scale).astype(BF) for a, d, t in zip(pgf, dgs, deltas)]
+        gqs = [(mm(a, k) + mm(b, kgv)).astype(BF) for a, b, k in zip(sls, sgs, ks)]
+        dkl = [tn(a, q) for a, q in zip(sls, qs)]
+        dks = tn(jnp.concatenate(sgs, 0), jnp.concatenate(qs, 0))
+        for h in (0, 1):
+            gt[out_box(tiles[h], 0)] = gqs[h]
+        for h in (0, 1):
+            dkp[wins[h]] += dkl[h]
+            dvp[wins[h]] += dvl[h]
+        dkg[...] += dks
+        dvg[...] += dvs
 
     def home_q(j):
         return remote(box(j, 0), spot(0, 1).at[0], dssem.at[j], drsem.at[me], chip(j))
@@ -640,8 +672,7 @@
     @pl.loop(1, 9)
     def _(n):
         j = lax.rem(me + n, 8)
-        backward(2 * j)
-        backward(2 * j + 1)
+        backward(j)
 
         @pl.when(n < 8)
         def _():
@@ -689,6 +720,10 @@
         home_q(j).wait_send()
         remote(box(j, 0), spot(0, 1).at[0], dssem.at[j], drsem.at[j], sib).wait_recv()
     home_q_own.wait()
+    turn(0)
+    for n in range(8):
+        piece(red_q, tok, n, 0, 1)
+    red_q.start_y()
     for cp in home_kv:
         cp.wait()
     home_kv_own.wait()
@@ -729,20 +764,16 @@
                 pr[o, rows, cols] = total.astype(BF)
 
     tokens_part(0)
-    tokens_part(1)
+    turn(1)
+    turn(2)
     to_sib[0].wait_recv()
     sum_rows(0)
     xc[0].start()
     xc[1].start()
-    turn(0)
-    for n in range(8):
-        piece(red_q, tok, n, 0, 1)
-    red_q.start_y()
-    tokens_part(2)
-    turn(1)
-    turn(2)
     for n in range(4):
         piece(red_v, tok, n, 1, 2)
+    tokens_part(1)
+    tokens_part(2)
     red_o.dep_z()
     red_o.dep_y()
     for n in range(4, 8):

time: 193 us -> 187 us (0.969)
  Pallas kernels: 185 us -> 179 us
    pallas_call x1, Pallas kernels: 185 us -> 179 us  [on_device(): pl.pallas_call(kernel, out_shape=(jax.ShapeDtypeStruct((ROWS, D), BF), sq...]
where the time goes in v4:
time: 187 us; the launch traced here: 186 us
  Pallas kernels  179 us (96%)
  local copies, waits for them, and re-layouts  6.56 us (4%)
    pallas_call x1, Pallas kernels, on_device(): pl.pallas_call(kernel, out_shape=(jax.ShapeDtypeStruct((ROWS, D), BF), sq...  179 us
    unnamed x14, local copies, waits for them, and re-layouts  6.56 us

profile of v4, /device:TPU:1, one launch (start us, length us, event | category | flops | bytes accessed | tf_op | source)
XLA Modules:
  0.0 185.9 jit_solution(10271609591143811561)
XLA Ops:
  0.6 1.4 copy.13.pat
  2.0 178.7 %shard_map.119 = (bf16[128,4096]{1,0:T(8,128)(2,1)}, f32[256,256]{1,0:T(8,128)}, f32[256,256]{1,0:T(8,128)}, f32[256,256]{1,0:T(8,128)}, f32[256,256]{1,0:T(8,128)}) custom-call(s32[8,2,2]{2,1,0:T(2,128)} %copy.13.pat, s32[8,128]{1,0:T(8,128)} %gpos.1, bf16[128,4096]{1,0:T(8,128)(2,1)} %bitcast.4, bf16[128,4096]{1,0:T(8,128)(2,1)} %bitcast.5, ...), custom_call_target="tpu_custom_call" | custom-call | flops 24999999488 | bytes 62914560 | tf_op jit(solution)/shard_map/pallas_call | solution.py:874
  180.7 0.0 copy-start.3
  180.7 0.0 copy-start.2
  180.7 0.0 copy-start.1
  180.7 0.0 copy-start
  180.7 2.4 %copy.19 = bf16[1,128,4096]{2,1,0:T(8,128)(2,1)} copy(bf16[1,128,4096]{2,1,0:T(8,128)(2,1)} %bitcast.3) | data formatting | bytes 2097152
  183.1 0.0 copy-done.3
  183.1 0.7 copy.20
  183.8 0.0 copy-done.2
  183.8 0.7 copy.21
  184.5 0.0 copy-done.1
  184.5 0.7 copy.22
  185.2 0.0 copy-done
  185.2 0.7 copy.23
Async XLA Ops:
  180.7 2.4 %copy-start.3 = (f32[256,256]{1,0:T(8,128)S(1)}, f32[256,256]{1,0:T(8,128)}, u32[]{:S(2)}) copy-start(f32[256,256]{1,0:T(8,128)} %get-tuple-element.21) | copy-start | bytes 786436
  180.7 3.1 %copy-start.2 = (f32[256,256]{1,0:T(8,128)S(1)}, f32[256,256]{1,0:T(8,128)}, u32[]{:S(2)}) copy-start(f32[256,256]{1,0:T(8,128)} %get-tuple-element.22) | copy-start | bytes 786436
  180.7 3.8 %copy-start.1 = (f32[256,256]{1,0:T(8,128)S(1)}, f32[256,256]{1,0:T(8,128)}, u32[]{:S(2)}) copy-start(f32[256,256]{1,0:T(8,128)} %get-tuple-element.23) | copy-start | bytes 786436
  180.7 4.5 %copy-start = (f32[256,256]{1,0:T(8,128)S(1)}, f32[256,256]{1,0:T(8,128)}, u32[]{:S(2)}) copy-start(f32[256,256]{1,0:T(8,128)} %get-tuple-element.24) | copy-start | bytes 786436

commit v5 on v4

--- a/solution.py
+++ b/solution.py
@@ -764,18 +764,20 @@
                 pr[o, rows, cols] = total.astype(BF)
 
     tokens_part(0)
-    turn(1)
-    turn(2)
+    tokens_part(1)
     to_sib[0].wait_recv()
     sum_rows(0)
     xc[0].start()
     xc[1].start()
-    for n in range(4):
+    tokens_part(2)
+    turn(1)
+    turn(2)
+    for n in range(0, 4):
         piece(red_v, tok, n, 1, 2)
-    tokens_part(1)
-    tokens_part(2)
     red_o.dep_z()
     red_o.dep_y()
+    red_q.dep_z()
+    red_q.dep_y()
     for n in range(4, 8):
         piece(red_v, tok, n, 1, 2)
     red_v.start_y()
@@ -787,13 +789,11 @@
     xc[1].wait_recv()
     sum_rows(2, 1)
     xc[3].start()
-    red_q.dep_z()
-    red_q.dep_y()
+    red_v.dep_z()
+    red_v.dep_y()
     red_o.mid_z()
     red_o.mid_y()
     tokens_part(3)
-    red_v.dep_z()
-    red_v.dep_y()
     red_o.last_z()
     red_o.last_y()
     red_q.mid_z()

time: 187 us -> 186 us (level)
  no operation moved by 1% of the time
where the time goes in v5:
time: 186 us; the launch traced here: 185 us
  Pallas kernels  178 us (96%)
  local copies, waits for them, and re-layouts  6.56 us (4%)
    pallas_call x1, Pallas kernels, on_device(): pl.pallas_call(kernel, out_shape=(jax.ShapeDtypeStruct((ROWS, D), BF), sq...  178 us
    unnamed x14, local copies, waits for them, and re-layouts  6.56 us

profile of v5, /device:TPU:1, one launch (start us, length us, event | category | flops | bytes accessed | tf_op | source)
XLA Modules:
  0.0 185.2 jit_solution(9466539088243749612)
XLA Ops:
  0.6 1.4 copy.13.pat
  2.0 178.0 %shard_map.119 = (bf16[128,4096]{1,0:T(8,128)(2,1)}, f32[256,256]{1,0:T(8,128)}, f32[256,256]{1,0:T(8,128)}, f32[256,256]{1,0:T(8,128)}, f32[256,256]{1,0:T(8,128)}) custom-call(s32[8,2,2]{2,1,0:T(2,128)} %copy.13.pat, s32[8,128]{1,0:T(8,128)} %gpos.1, bf16[128,4096]{1,0:T(8,128)(2,1)} %bitcast.4, bf16[128,4096]{1,0:T(8,128)(2,1)} %bitcast.5, ...), custom_call_target="tpu_custom_call" | custom-call | flops 24999999488 | bytes 62914560 | tf_op jit(solution)/shard_map/pallas_call | solution.py:874
  180.0 0.0 copy-start.3
  180.0 0.0 copy-start.2
  180.0 0.0 copy-start.1
  180.0 0.0 copy-start
  180.0 2.4 %copy.19 = bf16[1,128,4096]{2,1,0:T(8,128)(2,1)} copy(bf16[1,128,4096]{2,1,0:T(8,128)(2,1)} %bitcast.3) | data formatting | bytes 2097152
  182.4 0.0 copy-done.3
  182.4 0.7 copy.20
  183.1 0.0 copy-done.2
  183.1 0.7 copy.21
  183.8 0.0 copy-done.1
  183.8 0.7 copy.22
  184.5 0.0 copy-done
  184.5 0.7 copy.23
Async XLA Ops:
  180.0 2.4 %copy-start.3 = (f32[256,256]{1,0:T(8,128)S(1)}, f32[256,256]{1,0:T(8,128)}, u32[]{:S(2)}) copy-start(f32[256,256]{1,0:T(8,128)} %get-tuple-element.21) | copy-start | bytes 786436
  180.0 3.1 %copy-start.2 = (f32[256,256]{1,0:T(8,128)S(1)}, f32[256,256]{1,0:T(8,128)}, u32[]{:S(2)}) copy-start(f32[256,256]{1,0:T(8,128)} %get-tuple-element.22) | copy-start | bytes 786436
  180.0 3.8 %copy-start.1 = (f32[256,256]{1,0:T(8,128)S(1)}, f32[256,256]{1,0:T(8,128)}, u32[]{:S(2)}) copy-start(f32[256,256]{1,0:T(8,128)} %get-tuple-element.23) | copy-start | bytes 786436
  180.0 4.5 %copy-start = (f32[256,256]{1,0:T(8,128)S(1)}, f32[256,256]{1,0:T(8,128)}, u32[]{:S(2)}) copy-start(f32[256,256]{1,0:T(8,128)} %get-tuple-element.24) | copy-start | bytes 786436

commit v6 on v5

--- a/solution.py
+++ b/solution.py
@@ -680,29 +680,32 @@
 
     home_q_own.start()
 
-    def home(sems, t0, n):
-        s, d = sems
-        return [
-            remote(boxes(j, t0, n), spot(t0, n), s.at[k], d.at[k], where) for k, (j, where) in enumerate(peers)
-        ]
-
     def split(a):
         high = a.astype(BF)
         return high, (a - high.astype(F32)).astype(BF)
 
     both = jnp.concatenate([jnp.concatenate(split(dkg[...]), 0), jnp.concatenate(split(dvg[...]), 0)], 1)
 
-    @pl.loop(0, 16)
-    def _(i):
+    def finish(i):
         inner = pl.ds(al(i * 128 + BLOCK, 64), 128)
         put = (pos == i * 128 + sub).astype(F32).astype(BF)
         extra = mm(jnp.concatenate([put, put], 1), both)
         gt[out_box(i, 1)] = (dkp[inner] + extra[:, :128]).astype(BF)
         gt[out_box(i, 2)] = (dvp[inner] + extra[:, 128:]).astype(BF)
 
-    home_kv = home((essem, ersem), 1, 2)
-    for cp in home_kv:
-        cp.start()
+    def home_kv(j):
+        return remote(boxes(j, 1, 2), spot(1, 2), essem.at[j], ersem.at[me], chip(j))
+
+    @pl.loop(1, 9)
+    def _(n):
+        j = lax.rem(me + n, 8)
+        finish(2 * j)
+        finish(2 * j + 1)
+
+        @pl.when(n < 8)
+        def _():
+            home_kv(j).start()
+
     home_kv_own = pltpu.make_async_copy(boxes(me, 1, 2), spot(1, 2), lsem.at[11])
     home_kv_own.start()
 
@@ -724,8 +727,10 @@
     for n in range(8):
         piece(red_q, tok, n, 0, 1)
     red_q.start_y()
-    for cp in home_kv:
-        cp.wait()
+    for n in range(1, 8):
+        j = lax.rem(me + n, 8)
+        home_kv(j).wait_send()
+        remote(boxes(j, 1, 2), spot(1, 2), essem.at[j], ersem.at[j], sib).wait_recv()
     home_kv_own.wait()
 
     part = cot
@@ -897,7 +902,7 @@
             *reduce_scratch(HALF_KV),
             dma((2, 9)), dma((2, 9)), dma((12,)), dma((8, 2)), dma((13,)), dma((8,)), dma((8,)),
             dma((8,)), dma((8,)), dma((8,)), dma((8,)), dma((7,)), dma((7,)), dma((8,)), dma((8,)),
-            dma((7,)), dma((7,)), dma((4,)), dma((4,)), dma((4,)), dma((4,)), dma((4,)), dma((4,)), dma((4,)),
+            dma((8,)), dma((8,)), dma((4,)), dma((4,)), dma((4,)), dma((4,)), dma((4,)), dma((4,)), dma((4,)),
         ],
         compiler_params=pltpu.CompilerParams(
             collective_id=0, has_side_effects=True, vmem_limit_bytes=63 << 20

time: 186 us -> 186 us (level)
  no operation moved by 1% of the time
where the time goes in v6:
time: 186 us; the launch traced here: 185 us
  Pallas kernels  178 us (96%)
  local copies, waits for them, and re-layouts  6.56 us (4%)
    pallas_call x1, Pallas kernels, on_device(): pl.pallas_call(kernel, out_shape=(jax.ShapeDtypeStruct((ROWS, D), BF), sq...  178 us
    unnamed x14, local copies, waits for them, and re-layouts  6.56 us

profile of v6, /device:TPU:1, one launch (start us, length us, event | category | flops | bytes accessed | tf_op | source)
XLA Modules:
  0.0 185.3 jit_solution(15112292939136841881)
XLA Ops:
  0.6 1.4 copy.13.pat
  2.0 178.0 %shard_map.119 = (bf16[128,4096]{1,0:T(8,128)(2,1)}, f32[256,256]{1,0:T(8,128)}, f32[256,256]{1,0:T(8,128)}, f32[256,256]{1,0:T(8,128)}, f32[256,256]{1,0:T(8,128)}) custom-call(s32[8,2,2]{2,1,0:T(2,128)} %copy.13.pat, s32[8,128]{1,0:T(8,128)} %gpos.1, bf16[128,4096]{1,0:T(8,128)(2,1)} %bitcast.4, bf16[128,4096]{1,0:T(8,128)(2,1)} %bitcast.5, ...), custom_call_target="tpu_custom_call" | custom-call | flops 24999999488 | bytes 62914560 | tf_op jit(solution)/shard_map/pallas_call | solution.py:879
  180.0 0.0 copy-start.3
  180.0 0.0 copy-start.2
  180.0 0.0 copy-start.1
  180.1 0.0 copy-start
  180.1 2.4 %copy.19 = bf16[1,128,4096]{2,1,0:T(8,128)(2,1)} copy(bf16[1,128,4096]{2,1,0:T(8,128)(2,1)} %bitcast.3) | data formatting | bytes 2097152
  182.4 0.0 copy-done.3
  182.4 0.7 copy.20
  183.1 0.0 copy-done.2
  183.1 0.7 copy.21
  183.9 0.0 copy-done.1
  183.9 0.7 copy.22
  184.6 0.0 copy-done
  184.6 0.7 copy.23
Async XLA Ops:
  180.0 2.4 %copy-start.3 = (f32[256,256]{1,0:T(8,128)S(1)}, f32[256,256]{1,0:T(8,128)}, u32[]{:S(2)}) copy-start(f32[256,256]{1,0:T(8,128)} %get-tuple-element.21) | copy-start | bytes 786436
  180.0 3.1 %copy-start.2 = (f32[256,256]{1,0:T(8,128)S(1)}, f32[256,256]{1,0:T(8,128)}, u32[]{:S(2)}) copy-start(f32[256,256]{1,0:T(8,128)} %get-tuple-element.22) | copy-start | bytes 786436
  180.0 3.8 %copy-start.1 = (f32[256,256]{1,0:T(8,128)S(1)}, f32[256,256]{1,0:T(8,128)}, u32[]{:S(2)}) copy-start(f32[256,256]{1,0:T(8,128)} %get-tuple-element.23) | copy-start | bytes 786436
  180.1 4.5 %copy-start = (f32[256,256]{1,0:T(8,128)S(1)}, f32[256,256]{1,0:T(8,128)}, u32[]{:S(2)}) copy-start(f32[256,256]{1,0:T(8,128)} %get-tuple-element.24) | copy-start | bytes 786436
